TPU v7x, 32 devices: a whole 2x2x4 slice. The times are simulated.
32 devices in a mesh: batch: 8 (over z, y), tm: 4 (over x, core).
Axes of the slice: x: 2, y: 2, z: 4, core: 2. Of those that a mesh axis runs over, the one named last changes fastest.
Arguments:
- features: float32 [16, 1024, 512], P('batch', 'tm'), may hold values from -6 to 6
- dense_input: float32 [16, 1024, 2560], P('batch', 'tm'), may hold values from -6 to 6
- lengths: int32 [16], P('batch'), may hold values from 256 to 1024, as said below
- time_span: int32 [16, 2], P('batch'), may hold values from 0 to 960, as said below
- freq_span: int32 [16, 2], P('batch'), may hold values from 0 to 448, as said below
- w_first: bfloat16 [21, 512, 640], replicated, may hold values from -0.0625 to 0.0625
- w_rest: bfloat16 [4, 21, 640, 640], replicated, may hold values from -0.0546875 to 0.0546875
- w_res: bfloat16 [2560, 640], replicated, may hold values from -0.125 to 0.125
- norm_gains: float32 [6, 640], replicated, may hold values from 0.5 to 1.5
- norm_biases: float32 [6, 640], replicated, may hold values from -0.5 to 0.5
- cotangent: float32 [16, 1024, 640], P('batch', 'tm'), may hold values from -8 to 8
Outputs:
- result: float32 [16, 1024, 640], P('batch', 'tm')
- grad_features: float32 [16, 1024, 512], P('batch', 'tm')
- grad_dense: float32 [16, 1024, 2560], P('batch', 'tm')
- grad_first: float32 [21, 512, 640], P(None, 'tm', 'batch')
- grad_rest: float32 [4, 21, 640, 640], P(None, None, 'tm', 'batch')
- grad_res: float32 [2560, 640], P('tm', 'batch')
- grad_gains: float32 [6, 640], replicated
- grad_biases: float32 [6, 640], replicated
Inputs may be any that keep to these rules, and one draw needn't show every extreme that they name: `lengths`: of each 2 consecutive utterances one has all 1024 frames; every utterance has 256 frames or more. `time_span`: column 0 is the first masked frame, column 1 the mask's width, 1 to 64. `freq_span`: column 0 is the first masked channel, column 1 the mask's width, 1 to 64.
All inputs are finite; a program needn't handle non-finite values.
Results may differ from a plain program's by a relative error of at most 0.023.
Values may be sent and summed in bfloat16 or wider, within the bound.
No kernel may reach another device: no remote copies, remote signals or barrier semaphores. Data moves between devices by JAX's collectives and lax.ppermute only.
A program may use at most 512 MiB of HBM per device.

v0:
```python
import jax
import jax.numpy as jnp
from jax import lax
from jax.sharding import PartitionSpec as P

EPSILON = 1e-05


def padded_2(block, sides, width):
    for axis, dim in sides:
        count = lax.axis_size(axis)
        forward = [(i, i + 1) for i in range(count - 1)]
        backward = [(target, source) for source, target in forward]
        low = lax.ppermute(
            lax.slice_in_dim(block, block.shape[dim] - width, None, axis=dim), axis, forward
        )
        high = lax.ppermute(lax.slice_in_dim(block, 0, width, axis=dim), axis, backward)
        block = jnp.concatenate([low, block, high], axis=dim)
    return block


def silu_slope(hidden):
    logistic = jax.nn.sigmoid(hidden)
    return logistic * (1.0 + hidden * (1.0 - logistic))


def span_keep(span_cols, positions):
    inside = (positions[None, :] >= span_cols[:, 0:1]) & (
        positions[None, :] < span_cols[:, 0:1] + span_cols[:, 1:2]
    )
    return 1.0 - inside.astype(jnp.float32)


def shifted_taps(padded, kernel_len, frames_here, reverse):
    if reverse:
        return jnp.stack(
            [
                padded[:, kernel_len - 1 - tap_index : kernel_len - 1 - tap_index + frames_here]
                for tap_index in range(kernel_len)
            ],
            axis=2,
        )
    return jnp.stack(
        [padded[:, tap_index : tap_index + frames_here] for tap_index in range(kernel_len)], axis=2
    )


def body(
    features,
    dense_input,
    lengths,
    time_span,
    freq_span,
    w_first,
    w_rest,
    w_res,
    norm_gains,
    norm_biases,
    cotangent,
):
    utterances, frames_here, in_channels = features.shape
    kernel_len = w_first.shape[0]
    half_kernel = kernel_len // 2
    layers = [w_first] + [w_rest[sub_block] for sub_block in range(w_rest.shape[0])]
    block_count = len(layers)
    offset = lax.axis_index("tm") * frames_here
    frames = offset + jnp.arange(frames_here, dtype=jnp.int32)
    valid_mask = (frames[None, :] < lengths[:, None]).astype(jnp.float32)[:, :, None]
    channels = jnp.arange(in_channels, dtype=jnp.int32)
    keep_mask = (
        valid_mask
        * span_keep(time_span, frames)[:, :, None]
        * span_keep(freq_span, channels)[:, None, :]
    )
    start_low = (features * keep_mask).astype(jnp.bfloat16)
    dense_low = (dense_input * valid_mask).astype(jnp.bfloat16)
    local_count = jnp.sum(valid_mask)

    def forward_halo(hidden):
        return padded_2(hidden, (("tm", 1),), half_kernel)

    def moments(linear):
        return jnp.stack(
            [
                jnp.sum(linear * valid_mask, axis=(0, 1)),
                jnp.sum(linear * linear * valid_mask, axis=(0, 1)),
            ]
        )

    def back_moments(upstream, scaled):
        return jnp.stack([jnp.sum(upstream * scaled, axis=(0, 1)), jnp.sum(upstream, axis=(0, 1))])

    def normalize(linear, summed, counted, sub_block):
        average = summed[0] / counted
        inv_std = lax.rsqrt(summed[1] / counted - average * average + EPSILON)
        scaled = (linear - average) * inv_std
        return (scaled * norm_gains[sub_block] + norm_biases[sub_block], scaled, inv_std)

    def norm_back(upstream, scaled, inv_std, sub_block, grad_sums, counted):
        return (
            valid_mask
            * norm_gains[sub_block]
            * inv_std
            * (upstream - grad_sums[1] / counted - scaled * grad_sums[0] / counted)
        )

    def reduce_back(local_sums):
        return lax.psum(local_sums, ("batch", "tm"))

    def reduce_weights(local_grad):
        shared = lax.psum_scatter(
            local_grad.astype(jnp.bfloat16), "batch", scatter_dimension=2, tiled=True
        )
        return lax.psum_scatter(shared, "tm", scatter_dimension=1, tiled=True).astype(jnp.float32)

    def run(known_stats):
        hidden = start_low
        padded_all, scaled_all, inv_all, normed_all, totals = ([], [], [], [], [])
        for sub_block in range(block_count):
            padded = forward_halo(hidden)
            linear = jnp.einsum(
                "utki,kic->utc",
                shifted_taps(padded, kernel_len, frames_here, False),
                layers[sub_block],
                preferred_element_type=jnp.float32,
            )
            if known_stats is None:
                local_moments = moments(linear)
                summed, counted = lax.psum((local_moments, local_count), ("batch", "tm"))
            else:
                summed, counted = known_stats[sub_block]
            totals.append((summed, counted))
            normed, scaled, inv_std = normalize(linear, summed, counted, sub_block)
            padded_all.append(padded)
            scaled_all.append(scaled)
            inv_all.append(inv_std)
            normed_all.append(normed)
            if sub_block + 1 < block_count:
                hidden = (jax.nn.silu(normed) * valid_mask).astype(jnp.bfloat16)
        return (padded_all, scaled_all, inv_all, normed_all, totals)

    padded_all, scaled_all, inv_all, normed_all, totals = run(None)
    counted = totals[0][1]
    branch_linear = jnp.einsum("utd,dc->utc", dense_low, w_res, preferred_element_type=jnp.float32)
    branch_summed = lax.psum(moments(branch_linear), ("batch", "tm"))
    branch_normed, branch_scaled, branch_inv = normalize(
        branch_linear, branch_summed, counted, block_count
    )
    joined = normed_all[-1] + branch_normed
    result = jax.nn.silu(joined) * valid_mask
    padded_all, scaled_all, inv_all, normed_all, totals = run(totals)
    upstream = cotangent * valid_mask * silu_slope(joined)
    final_sums = reduce_back(
        jnp.concatenate(
            [back_moments(upstream, scaled_all[-1]), back_moments(upstream, branch_scaled)], axis=0
        )
    )
    gain_grads = [None] * (block_count + 1)
    bias_grads = [None] * (block_count + 1)
    gain_grads[block_count - 1] = final_sums[0]
    bias_grads[block_count - 1] = final_sums[1]
    gain_grads[block_count] = final_sums[2]
    bias_grads[block_count] = final_sums[3]
    branch_grad = norm_back(
        upstream, branch_scaled, branch_inv, block_count, final_sums[2:4], counted
    ).astype(jnp.bfloat16)
    grad_dense = (
        jnp.einsum("utc,dc->utd", branch_grad, w_res, preferred_element_type=jnp.float32)
        * valid_mask
    )
    grad_res = reduce_weights(
        jnp.einsum("utd,utc->dc", dense_low, branch_grad, preferred_element_type=jnp.float32)[None]
    )[0]
    linear_grad = norm_back(
        upstream, scaled_all[-1], inv_all[-1], block_count - 1, final_sums[0:2], counted
    ).astype(jnp.bfloat16)
    weight_grads = [None] * block_count
    grad_features = None
    for sub_block in range(block_count - 1, -1, -1):
        tap_stack = shifted_taps(padded_all[sub_block], kernel_len, frames_here, False)
        weight_grads[sub_block] = reduce_weights(
            jnp.einsum("utki,utc->kic", tap_stack, linear_grad, preferred_element_type=jnp.float32)
        )
        widened = padded_2(linear_grad, (("tm", 1),), half_kernel)
        input_grad = jnp.einsum(
            "utkc,kic->uti",
            shifted_taps(widened, kernel_len, frames_here, True),
            layers[sub_block],
            preferred_element_type=jnp.float32,
        )
        if sub_block == 0:
            grad_features = input_grad * keep_mask
        else:
            upstream = input_grad * valid_mask * silu_slope(normed_all[sub_block - 1])
            grad_sums = reduce_back(back_moments(upstream, scaled_all[sub_block - 1]))
            gain_grads[sub_block - 1] = grad_sums[0]
            bias_grads[sub_block - 1] = grad_sums[1]
            linear_grad = norm_back(
                upstream,
                scaled_all[sub_block - 1],
                inv_all[sub_block - 1],
                sub_block - 1,
                grad_sums,
                counted,
            ).astype(jnp.bfloat16)
    return (
        result,
        grad_features,
        grad_dense,
        weight_grads[0],
        jnp.stack(weight_grads[1:]),
        grad_res,
        jnp.stack(gain_grads),
        jnp.stack(bias_grads),
    )


def solution(mesh):
    placed = (
        P("batch", "tm", None),
        P("batch", "tm", None),
        P("batch"),
        P("batch", None),
        P("batch", None),
        P(),
        P(),
        P(),
        P(),
        P(),
        P("batch", "tm", None),
    )
    return jax.shard_map(
        body,
        mesh=mesh,
        in_specs=placed,
        out_specs=(
            P("batch", "tm", None),
            P("batch", "tm", None),
            P("batch", "tm", None),
            P(None, "tm", "batch"),
            P(None, None, "tm", "batch"),
            P("tm", "batch"),
            P(),
            P(),
        ),
        check_vma=False,
    )
```

profile of v0, /device:TPU:0, one launch (start us, length us, event | category | flops | bytes accessed | tf_op | source)
XLA Modules:
  0.0 2510.5 jit_solution(1304072259176949300)
XLA Ops:
  20.5 17.2 multiply_reduce_fusion.17
  37.8 44.1 %all-reduce.1 = (f32[2,640]{1,0:T(2,128)S(1)}, f32[]{:T(128)}) all-reduce(f32[2,640]{1,0:T(2,128)S(1)} %pad_maximum_fusion.21, f32[]{:T(128)} %fusion.676), channel_id=1, replica_groups=mesh['batch'=8,'tm'=4] {'batch','tm'}, use_global_device_ids=true, to_apply=%region_2.0 | all-reduce | flops 1281 | bytes 10248 | tf_op jit(solution)/shard_map/psum | solution.py:129
  108.7 19.8 multiply_reduce_fusion.15
  128.5 43.3 %psum.98 = f32[2,640]{1,0:T(2,128)S(1)} all-reduce(f32[2,640]{1,0:T(2,128)S(1)} %pad_maximum_fusion.22), channel_id=1, replica_groups=mesh['batch'=8,'tm'=4] {'batch','tm'}, use_global_device_ids=true, to_apply=%region_7.8 | all-reduce | flops 1280 | bytes 10240 | tf_op jit(solution)/shard_map/psum | solution.py:129
  198.9 19.9 multiply_reduce_fusion.13
  218.8 42.9 %psum.99 = f32[2,640]{1,0:T(2,128)S(1)} all-reduce(f32[2,640]{1,0:T(2,128)S(1)} %pad_maximum_fusion.23), channel_id=1, replica_groups=mesh['batch'=8,'tm'=4] {'batch','tm'}, use_global_device_ids=true, to_apply=%region_10.11 | all-reduce | flops 1280 | bytes 10240 | tf_op jit(solution)/shard_map/psum | solution.py:129
  288.4 19.9 multiply_reduce_fusion.11
  308.3 43.2 %psum.100 = f32[2,640]{1,0:T(2,128)S(1)} all-reduce(f32[2,640]{1,0:T(2,128)S(1)} %pad_maximum_fusion.24), channel_id=1, replica_groups=mesh['batch'=8,'tm'=4] {'batch','tm'}, use_global_device_ids=true, to_apply=%region_13.14 | all-reduce | flops 1280 | bytes 10240 | tf_op jit(solution)/shard_map/psum | solution.py:129
  384.1 20.0 multiply_reduce_fusion.9
  404.2 43.1 %all-reduce = (f32[2,640]{1,0:T(2,128)S(1)}, f32[2,640]{1,0:T(2,128)S(1)}) all-reduce(f32[2,640]{1,0:T(2,128)S(1)} %pad_maximum_fusion.26, f32[2,640]{1,0:T(2,128)S(1)} %pad_maximum_fusion.25), channel_id=1, replica_groups=mesh['batch'=8,'tm'=4] {'batch','tm'}, use_global_device_ids=true, to_apply=%region_19.20 | all-reduce | flops 2560 | bytes 20480 | tf_op jit(solution)/shard_map/psum | solution.py:145
  452.8 40.7 %psum.103 = f32[4,640]{1,0:T(4,128)S(1)} all-reduce(f32[4,640]{1,0:T(4,128)S(1)} %pad_maximum_fusion.20), channel_id=1, replica_groups=mesh['batch'=8,'tm'=4] {'batch','tm'}, use_global_device_ids=true, to_apply=%region_23.24 | all-reduce | flops 2560 | bytes 20480 | tf_op jit(solution)/shard_map/psum | solution.py:108
  524.6 19.4 multiply_reduce_fusion.3
  544.0 40.0 %psum.104 = f32[2,640]{1,0:T(2,128)S(1)} all-reduce(f32[2,640]{1,0:T(2,128)S(1)} %pad_maximum_fusion.27), channel_id=1, replica_groups=mesh['batch'=8,'tm'=4] {'batch','tm'}, use_global_device_ids=true, to_apply=%region_26.27 | all-reduce | flops 1280 | bytes 10240 | tf_op jit(solution)/shard_map/psum | solution.py:108
  613.5 19.3 multiply_reduce_fusion.2
  632.9 40.2 %psum.105 = f32[2,640]{1,0:T(2,128)S(1)} all-reduce(f32[2,640]{1,0:T(2,128)S(1)} %pad_maximum_fusion.28), channel_id=1, replica_groups=mesh['batch'=8,'tm'=4] {'batch','tm'}, use_global_device_ids=true, to_apply=%region_29.30 | all-reduce | flops 1280 | bytes 10240 | tf_op jit(solution)/shard_map/psum | solution.py:108
  702.7 19.4 multiply_reduce_fusion.1
  722.1 40.0 %psum.106 = f32[2,640]{1,0:T(2,128)S(1)} all-reduce(f32[2,640]{1,0:T(2,128)S(1)} %pad_maximum_fusion.29), channel_id=1, replica_groups=mesh['batch'=8,'tm'=4] {'batch','tm'}, use_global_device_ids=true, to_apply=%region_32.33 | all-reduce | flops 1280 | bytes 10240 | tf_op jit(solution)/shard_map/psum | solution.py:108
  819.8 19.5 multiply_reduce_fusion
  839.4 41.6 %psum.107 = f32[2,640]{1,0:T(2,128)S(1)} all-reduce(f32[2,640]{1,0:T(2,128)S(1)} %pad_maximum_fusion.30), channel_id=1, replica_groups=mesh['batch'=8,'tm'=4] {'batch','tm'}, use_global_device_ids=true, to_apply=%region_35.36 | all-reduce | flops 1280 | bytes 10240 | tf_op jit(solution)/shard_map/psum | solution.py:108
  898.5 16.7 bitcast_convert_fusion
  915.4 16.4 bitcast_convert_fusion.1
  931.8 16.4 bitcast_convert_fusion.2
  948.5 16.5 bitcast_convert_fusion.3
  970.6 151.3 %reduce-scatter.25.cloned.1.call-done = bf16[21,512,80]{1,2,0:T(8,128)(2,1)} async-done(((bf16[21,512,640]{1,2,0:T(8,128)(2,1)}), bf16[21,512,80]{1,2,0:T(8,128)(2,1)}) %reduce-scatter.25.cloned.1.call-update) | async-done | bytes 1720336 | tf_op jit(solution)/shard_map/reduce_scatter | solution.py:111
  1132.2 281.1 %reduce-scatter.33.cloned.1.call-done = bf16[21,640,80]{1,2,0:T(8,128)(2,1)} async-done(((bf16[21,640,640]{1,2,0:T(8,128)(2,1)}), bf16[21,640,80]{1,2,0:T(8,128)(2,1)}) %reduce-scatter.33.cloned.1.call-update) | async-done | bytes 2150416 | tf_op jit(solution)/shard_map/reduce_scatter | solution.py:111
  1425.6 278.8 %reduce-scatter.31.cloned.1.call-done = bf16[21,640,80]{1,2,0:T(8,128)(2,1)} async-done(((bf16[21,640,640]{1,2,0:T(8,128)(2,1)}), bf16[21,640,80]{1,2,0:T(8,128)(2,1)}) %reduce-scatter.31.cloned.1.call-update) | async-done | bytes 2150416 | tf_op jit(solution)/shard_map/reduce_scatter | solution.py:111
  1716.7 278.9 %reduce-scatter.29.cloned.1.call-done = bf16[21,640,80]{1,2,0:T(8,128)(2,1)} async-done(((bf16[21,640,640]{1,2,0:T(8,128)(2,1)}), bf16[21,640,80]{1,2,0:T(8,128)(2,1)}) %reduce-scatter.29.cloned.1.call-update) | async-done | bytes 2150416 | tf_op jit(solution)/shard_map/reduce_scatter | solution.py:111
  2026.2 261.1 %reduce-scatter.27.cloned.1.call-done = bf16[21,640,80]{1,2,0:T(8,128)(2,1)} async-done(((bf16[21,640,640]{1,2,0:T(8,128)(2,1)}), bf16[21,640,80]{1,2,0:T(8,128)(2,1)}) %reduce-scatter.27.cloned.1.call-update) | async-done | bytes 2150416 | tf_op jit(solution)/shard_map/reduce_scatter | solution.py:111
  2350.7 28.6 %reduce-scatter.45.cloned.1.call-done = bf16[160,1680]{1,0:T(8,128)(2,1)} async-done(((bf16[640,1680]{1,0:T(8,128)(2,1)}), bf16[160,1680]{1,0:T(8,128)(2,1)}) %reduce-scatter.45.cloned.1.call-update) | async-done | bytes 537616
  2384.7 29.6 %reduce-scatter.43.cloned.1.call-done = bf16[160,1680]{1,0:T(8,128)(2,1)} async-done(((bf16[640,1680]{1,0:T(8,128)(2,1)}), bf16[160,1680]{1,0:T(8,128)(2,1)}) %reduce-scatter.43.cloned.1.call-update) | async-done | bytes 537616
  2419.8 29.9 %reduce-scatter.41.cloned.1.call-done = bf16[160,1680]{1,0:T(8,128)(2,1)} async-done(((bf16[640,1680]{1,0:T(8,128)(2,1)}), bf16[160,1680]{1,0:T(8,128)(2,1)}) %reduce-scatter.41.cloned.1.call-update) | async-done | bytes 537616
  2455.5 29.4 %reduce-scatter.39.cloned.1.call-done = bf16[160,1680]{1,0:T(8,128)(2,1)} async-done(((bf16[640,1680]{1,0:T(8,128)(2,1)}), bf16[160,1680]{1,0:T(8,128)(2,1)}) %reduce-scatter.39.cloned.1.call-update) | async-done | bytes 537616
  (499 shorter events, 466.5 us)
Async XLA Ops:
  7.2 957.9 %reduce-scatter.47.cloned.1.call-start = ((), (), s32[]{:S(2)}) async-start(), calls=%async_computation.23 | async-start | bytes 3686400
  11.5 7.7 collective-permute-start.1
  12.8 3.9 collective-permute-start
  84.4 2.9 collective-permute-start.2
  85.7 13.0 collective-permute-start.3
  174.4 3.1 collective-permute-start.4
  175.7 13.2 collective-permute-start.5
  264.2 2.8 collective-permute-start.6
  265.5 12.9 collective-permute-start.7
  354.0 8.6 collective-permute-start.8
  361.1 12.9 collective-permute-start.9
  499.2 4.3 collective-permute-start.10
  500.5 13.9 collective-permute-start.11
  588.0 4.5 collective-permute-start.12
  589.3 14.1 collective-permute-start.13
  677.1 4.6 collective-permute-start.14
  678.4 14.1 collective-permute-start.15
  767.1 30.6 %collective-permute-start.16 = (bf16[2,10,640]{2,1,0:T(8,128)(2,1)S(1)}, bf16[2,10,640]{2,1,0:T(8,128)(2,1)S(1)}, u32[]{:S(2)}, u32[]{:S(2)}) collective-permute-start(bf16[2,10,640]{2,1,0:T(8,128)(2,1)S(1)} %get-tuple-element.108), channel_id=1, source_target_pairs={{1,0},{2,1},{3,2},{5,4},{6,5},{7,6},{9,8},{10,9},{11,10},{13,12},{... | collective-permute-start | bytes 76808 | tf_op jit(solution)/shard_map/ppermute | solution.py:17
  794.1 327.9 %reduce-scatter.25.cloned.1.call-start = ((), (), s32[]{:S(2)}) async-start(), calls=%async_computation.12 | async-start | bytes 15482880 | tf_op jit(solution)/shard_map/reduce_scatter | solution.py:111
  794.1 15.5 collective-permute-start.17
  898.3 514.9 %reduce-scatter.33.cloned.1.call-start = ((), (), s32[]{:S(2)}) async-start(), calls=%async_computation.16 | async-start | bytes 19353600 | tf_op jit(solution)/shard_map/reduce_scatter | solution.py:111
  915.3 789.1 %reduce-scatter.31.cloned.1.call-start = ((), (), s32[]{:S(2)}) async-start(), calls=%async_computation.15 | async-start | bytes 19353600 | tf_op jit(solution)/shard_map/reduce_scatter | solution.py:111
  931.8 1063.7 %reduce-scatter.29.cloned.1.call-start = ((), (), s32[]{:S(2)}) async-start(), calls=%async_computation.14 | async-start | bytes 19353600 | tf_op jit(solution)/shard_map/reduce_scatter | solution.py:111
  948.3 1339.1 %reduce-scatter.27.cloned.1.call-start = ((), (), s32[]{:S(2)}) async-start(), calls=%async_computation.13 | async-start | bytes 19353600 | tf_op jit(solution)/shard_map/reduce_scatter | solution.py:111
  965.1 1368.3 %reduce-scatter.35.cloned.1.call-start = ((), (), s32[]{:S(2)}) async-start(), calls=%async_computation.17 | async-start | bytes 819200 | tf_op jit(solution)/shard_map/reduce_scatter | solution.py:114
  970.6 1373.2 %reduce-scatter.37.cloned.1.call-start = ((), (), s32[]{:S(2)}) async-start(), calls=%async_computation.18 | async-start | bytes 2293760
  1132.1 1247.1 %reduce-scatter.45.cloned.1.call-start = ((), (), s32[]{:S(2)}) async-start(), calls=%async_computation.22 | async-start | bytes 2867200
  1425.5 988.8 %reduce-scatter.43.cloned.1.call-start = ((), (), s32[]{:S(2)}) async-start(), calls=%async_computation.21 | async-start | bytes 2867200
  1716.6 733.1 %reduce-scatter.41.cloned.1.call-start = ((), (), s32[]{:S(2)}) async-start(), calls=%async_computation.20 | async-start | bytes 2867200
  2007.8 477.1 %reduce-scatter.39.cloned.1.call-start = ((), (), s32[]{:S(2)}) async-start(), calls=%async_computation.19 | async-start | bytes 2867200
  2008.7 11.4 collective-permute-start.18
  2015.7 291.2 %collective-permute-start.19 = (bf16[2,10,640]{2,1,0:T(8,128)(2,1)S(1)}, bf16[2,10,640]{2,1,0:T(8,128)(2,1)S(1)}, u32[]{:S(2)}, u32[]{:S(2)}) collective-permute-start(bf16[2,10,640]{2,1,0:T(8,128)(2,1)S(1)} %get-tuple-element.105), channel_id=1, source_target_pairs={{0,1},{1,2},{2,3},{4,5},{5,6},{6,7},{8,9},{9,10},{10,11},{12,13},{... | collective-permute-start | bytes 76808 | tf_op jit(solution)/shard_map/ppermute | solution.py:14
  (53 other events, 1205.7 us)
Sparse Core Ops, SparseCore 0:
  794.2 77.0 reduce-scatter.46
  898.4 223.4 reduce-scatter.24
  1125.8 287.3 reduce-scatter.32
  1417.0 287.3 reduce-scatter.30
  1708.1 287.3 reduce-scatter.28
  1999.3 288.0 reduce-scatter.26
  2289.8 21.5 reduce-scatter.34
  2314.0 29.7 reduce-scatter.36
  2346.6 32.6 reduce-scatter.44
  2381.6 32.6 reduce-scatter.42
  2417.1 32.6 reduce-scatter.40
  2452.2 32.6 reduce-scatter.38
where the time goes:
time: 2520 us; the launch traced here: 2510 us
  waiting for transfers between devices  1380 us (55%)
  blocking collectives  419 us (17%)
  matrix products  288 us (11%)
  other arithmetic  242 us (10%)
  local copies, waits for them, and re-layouts  131 us (5%)
  starting transfers between devices  39.3 us (2%)
    reduce_scatter x5, waiting for transfers between devices, reduce_weights(): lax.psum_scatter(local_grad.astype(jnp.bfloat16), 'batch', scatter_dimens...  1250 us
    psum x5, blocking collectives, reduce_back(): return lax.psum(local_sums, ('batch', 'tm'))  202 us
    unnamed x195, other arithmetic  183 us
    psum x4, blocking collectives, run(): summed, counted = lax.psum((local_moments, local_count), ('batch', 'tm'))  174 us
    unnamed x137, local copies, waits for them, and re-layouts  128 us
    unnamed x18, waiting for transfers between devices  125 us
    dot_general x5, matrix products, run(): jnp.einsum('utki,kic->utc', shifted_taps(padded, kernel_len, frames_here,...  96.8 us
    dot_general x5, matrix products, body(): jnp.einsum('utkc,kic->uti', shifted_taps(widened, kernel_len, frames_here...  93.8 us
  transfers between devices with their start and end apart: 32, of which 10 were waited for; matrix products, arithmetic and copies ran while one was open for 15% of the time, Pallas kernels for 0%

commit v1 on v0

v1 whole, which is shorter than its diff:
```python
import functools
import math

import jax
import jax.numpy as jnp
from jax import lax
from jax.experimental import pallas as pl
from jax.experimental.pallas import tpu as pltpu
from jax.sharding import Mesh, PartitionSpec as P

EPSILON = 1e-05
ALL = ("zh", "zl", "y", "x", "core")
DEPTH = ("zh", "zl")
BATCH = ("zh", "zl", "y")
TIME = ("x", "core")
LANES = 128
GROUP = 7
VMEM = pl.BlockSpec(memory_space=pltpu.VMEM)
SMEM = pl.BlockSpec(memory_space=pltpu.SMEM)
ANY = pl.BlockSpec(memory_space=pl.ANY)
PARAMS = pltpu.CompilerParams(vmem_limit_bytes=60 * 1024 * 1024)


def pieces_of(count):
    return -(-count // (8 * LANES)) * 8


def silu_slope(hidden):
    logistic = jax.nn.sigmoid(hidden)
    return logistic * (1.0 + hidden * (1.0 - logistic))


def plan(utterances, rows, kernel_len):
    phases = rows // LANES
    half = kernel_len // 2
    blocks = []
    for q in range(phases + kernel_len - 1):
        move = (q - half) // phases
        blocks.append((q - half - move * phases, move))
    reach = max(abs(move) for _, move in blocks)
    edge = -(-reach * utterances // 8) * 8
    return phases, blocks, edge


def valid_of(info, utterances, phases, phase, first, shape, axis):
    row = lax.broadcasted_iota(jnp.int32, shape, axis) + first
    frame = info[utterances] + (row // utterances) * phases + phase
    which = row % utterances
    length = jnp.full(shape, info[0], jnp.int32)
    for u in range(1, utterances):
        length = jnp.where(which == u, info[u], length)
    return ((frame >= 0) & (frame < length)).astype(jnp.float32)


def spread_blocks(blocks, utterances, axis, own, edges, put):
    for q, (phase, move) in enumerate(blocks):
        block = own[phase]
        if move:
            spot = lax.broadcasted_iota(jnp.int32, block.shape, axis)
            if move > 0:
                outside = spot < move * utterances
            else:
                outside = spot >= LANES + move * utterances
            block = jnp.where(outside, edges[phase], block)
            block = pltpu.roll(block, (-move * utterances) % LANES, axis)
        put(q, block)


def fetch(weight, base, buffer, sems, g):
    return pltpu.make_async_copy(weight.at[base + g], buffer.at[g], sems.at[g])


def flat_sums(came):
    summed = jnp.sum(came, axis=0)
    return jnp.concatenate([summed[i : i + 1] for i in range(summed.shape[0])], axis=1)


def put_sums(sums, rows_list):
    copies, pieces, _ = sums.shape
    at = 0
    for row in rows_list:
        for i in range(row.shape[1] // LANES):
            piece = row[:, i * LANES : (i + 1) * LANES]
            sums[:, at, :] = jnp.broadcast_to(piece, (copies, LANES))
            at += 1
    if at < pieces:
        sums[:, at:, :] = jnp.zeros((copies, pieces - at, LANES), jnp.float32)


def norm_terms(came, cout):
    summed = flat_sums(came)
    counted = summed[:, 2 * cout : 2 * cout + 1]
    average = summed[:, :cout] / counted
    inv = lax.rsqrt(summed[:, cout : 2 * cout] / counted - average * average + EPSILON)
    return average, inv, counted


def span_of(info, utterances, phases, phase, which, shape):
    at = utterances + 2 + 4 * which
    frame = info[utterances] + lax.broadcasted_iota(jnp.int32, shape, 0) * phases + phase
    channel = lax.broadcasted_iota(jnp.int32, shape, 1)
    inside = (frame >= info[at]) & (frame < info[at] + info[at + 1])
    inside |= (channel >= info[at + 2]) & (channel < info[at + 2] + info[at + 3])
    return ((frame < info[which]) & jnp.logical_not(inside)).astype(jnp.float32)


def frames_of(utterances, phases, phase, which):
    count = LANES // utterances
    return pl.ds(which * count * phases + phase, count, stride=phases)


def rows_of(utterances, first, which):
    return pl.ds(first + which, LANES // utterances, stride=utterances)


def lay(ref, stage):
    for j in range(stage.shape[0]):
        stage[j] = ref[:, j * LANES : (j + 1) * LANES]


def unlay(stage, ref):
    for j in range(stage.shape[0]):
        ref[:, j * LANES : (j + 1) * LANES] = stage[j]


def take(stage, index):
    return jnp.concatenate([stage[j, index, :] for j in range(stage.shape[0])], axis=1)


def give(stage, index, value):
    for j in range(stage.shape[0]):
        stage[j, index, :] = value[:, j * LANES : (j + 1) * LANES]


def forward_kernel(
    cfg, info, source, low, high, came, gain, bias, more, weight, linear, sums, low_out, high_out, flat, turned,
    buffer, haloed, sems, laid, staged,
):
    utterances, phases, blocks, edge, taps, base, normed = cfg
    groups = taps // GROUP
    rows, cin = source.shape
    cout = linear.shape[1]
    fetch(weight, base, buffer, sems, 0).start()
    if normed:
        average, inv, _ = norm_terms(came[...], cin)
        scale = inv * gain[...]
        shift = bias[...] - average * scale

    else:
        lay(source, laid)

    def activate(value, mask):
        if not normed:
            return value.astype(jnp.float32)
        value = value * scale + shift
        return value * jax.nn.sigmoid(value) * mask

    own, edges = [], []
    for p in range(phases):
        if normed:
            mask = valid_of(info, utterances, phases, p, 0, (LANES, 1), 0)
            block = activate(source[p * LANES : (p + 1) * LANES, :], mask).astype(jnp.bfloat16)
        else:
            for u in range(utterances):
                mask = span_of(info, utterances, phases, p, u, (LANES // utterances, cin))
                give(staged, rows_of(utterances, 0, u), take(laid, frames_of(utterances, phases, p, u)) * mask)
            block = take(staged, slice(None)).astype(jnp.bfloat16)
        own.append(block)
        flat[:, p * LANES : (p + 1) * LANES] = block.T
        mask = valid_of(info, utterances, phases, p, -edge, (edge, 1), 0)
        before = activate(low[p], mask)
        mask = valid_of(info, utterances, phases, p, LANES, (edge, 1), 0)
        after = activate(high[p], mask)
        middle = jnp.zeros((LANES - 2 * edge, cin), jnp.float32)
        edges.append(jnp.concatenate([after, middle, before], axis=0).astype(jnp.bfloat16))

    def put(q, block):
        haloed[q * LANES : (q + 1) * LANES, :] = block

    if groups > 1:
        fetch(weight, base, buffer, sems, 1).start()
    spread_blocks(blocks, utterances, 0, own, edges, put)
    linear[...] = jnp.zeros_like(linear)

    def step(g, carry):
        fetch(weight, base, buffer, sems, g).wait()

        @pl.when(g + 2 < groups)
        def _():
            fetch(weight, base, buffer, sems, g + 2).start()

        lhs = jnp.concatenate(
            [
                haloed[pl.ds(pl.multiple_of((g * GROUP + k) * LANES, LANES), rows), :]
                for k in range(GROUP)
            ],
            axis=1,
        )
        linear[...] += jnp.dot(lhs, buffer[g], preferred_element_type=jnp.float32)
        return carry

    lax.fori_loop(0, groups, step, 0)
    total = jnp.zeros((1, cout), jnp.float32)
    square = jnp.zeros((1, cout), jnp.float32)
    count = jnp.zeros((1, 1), jnp.float32)
    for p in range(phases):
        mask = valid_of(info, utterances, phases, p, 0, (LANES, 1), 0)
        block = linear[p * LANES : (p + 1) * LANES, :]
        masked = block * mask
        total += jnp.sum(masked, axis=0, keepdims=True)
        square += jnp.sum(masked * block, axis=0, keepdims=True)
        count += jnp.sum(mask, axis=0, keepdims=True)
        low_out[p] = block[LANES - edge :, :]
        high_out[p] = block[:edge, :]
        turned[:, p * LANES : (p + 1) * LANES] = block.astype(jnp.bfloat16).T
    terms = [total, square, jnp.broadcast_to(count, (1, LANES))]
    if more is not None:
        terms.append(more[...])
    put_sums(sums, terms)


def forward_conv(utterances, info, source, low, high, came, gain, bias, weight, layer, copies, more=None):
    _, taps, cin, cout = weight.shape
    rows = source.shape[0]
    phases, blocks, edge = plan(utterances, rows, taps)
    groups = taps // GROUP
    normed = came is not None
    if not normed:
        came = jnp.zeros((1, 8, LANES), jnp.float32)
        gain = bias = jnp.zeros((1, LANES), jnp.float32)
    cfg = (utterances, phases, blocks, edge, taps, layer * groups, normed)
    shape = jax.ShapeDtypeStruct
    terms = 2 * cout + LANES
    kernel = functools.partial(forward_kernel, cfg)
    extra = []
    if more is None:
        kernel = lambda *refs: forward_kernel(cfg, *refs[:7], None, *refs[7:])
    else:
        terms += more.shape[1]
        extra = [more]
    return pl.pallas_call(
        kernel,
        name="forward_conv",
        out_shape=(
            shape((rows, cout), jnp.float32),
            shape((copies, pieces_of(terms), LANES), jnp.float32),
            shape((phases, edge, cout), jnp.float32),
            shape((phases, edge, cout), jnp.float32),
            shape((cin, rows), jnp.bfloat16),
            shape((cout, rows), jnp.bfloat16),
        ),
        in_specs=[SMEM] + [VMEM] * (6 + len(extra)) + [ANY],
        out_specs=(VMEM,) * 6,
        scratch_shapes=[
            pltpu.VMEM((groups, GROUP * cin, cout), jnp.bfloat16),
            pltpu.VMEM((len(blocks) * LANES, cin), jnp.bfloat16),
            pltpu.SemaphoreType.DMA((groups,)),
            pltpu.VMEM((1 if normed else cin // LANES, 8 if normed else rows, LANES), jnp.float32),
            pltpu.VMEM((cin // LANES, LANES, LANES), jnp.float32),
        ],
        compiler_params=PARAMS,
        cost_estimate=pl.CostEstimate(
            flops=2 * taps * rows * cin * cout, bytes_accessed=2 * taps * cin * cout, transcendentals=0
        ),
    )(info, source, low, high, came, gain, bias, *extra, weight.reshape(-1, GROUP * cin, cout))


def columns_of(rows_list):
    count = len(rows_list)
    width = rows_list[0].shape[1]
    stacked = jnp.concatenate(
        rows_list + [jnp.zeros((LANES - count, width), jnp.float32)], axis=0
    )
    return stacked.T


def put_grad(out, value, table):
    if len(out.shape) == 2:
        out[...] = value
        return
    cols = out.shape[3]
    for g, blocks in enumerate(table):
        for k, block in enumerate(blocks):
            for x in range(out.shape[1]):
                out[g, x, k] = value[block * cols : (block + 1) * cols]


def backward_kernel(
    cfg, info, up, linear, low_up, high_up, low_lin, high_lin, came, came_up, gain, before, came_before,
    gain_before, bias_before, weight, grad, next_up, sums, low_out, high_out, row, buffer, haloed, sems, staged,
    whole, laid,
):
    utterances, phases, blocks, edge, taps, base, last, table = cfg
    groups = taps // GROUP
    cout, rows = up.shape
    cin = weight.shape[2]
    fetch(weight, base, buffer, sems, 0).start()
    average, inv, counted = norm_terms(came[...], cout)
    summed = flat_sums(came_up[...])
    grad_gain, grad_bias = summed[:, :cout], summed[:, cout : 2 * cout]
    row[...] = summed[:, : 2 * cout]
    keep_up = gain[...] * inv
    keep_lin = -keep_up * inv * grad_gain / counted
    rest = -keep_up * grad_bias / counted - keep_lin * average
    vectors = [keep_up, keep_lin, rest]
    if not last:
        average_b, inv_b, _ = norm_terms(came_before[...], cin)
        scale = inv_b * gain_before[...]
        vectors += [scale, bias_before[...] - average_b * scale, inv_b, -average_b * inv_b]
    columns = columns_of(vectors)

    def column(r):
        return columns[:, r : r + 1]

    pieces = []
    for p in range(phases):
        for first, up_edge, lin_edge in ((-edge, low_up, low_lin), (LANES, high_up, high_lin)):
            mask = valid_of(info, utterances, phases, p, first, (edge, 1), 0)
            pieces.append(mask * (up_edge[p] * keep_up + lin_edge[p] * keep_lin + rest))
    pieces.append(jnp.zeros((LANES - 2 * phases * edge, cout), jnp.float32))
    side = jnp.concatenate(pieces, axis=0).T
    own, edges, grads = [], [], []
    spot = lax.broadcasted_iota(jnp.int32, (cout, LANES), 1)
    for p in range(phases):
        cut = slice(p * LANES, (p + 1) * LANES)
        mask = valid_of(info, utterances, phases, p, 0, (1, LANES), 1)
        block = mask * (up[:, cut] * column(0) + linear[:, cut].astype(jnp.float32) * column(1) + column(2))
        block = block.astype(jnp.bfloat16)
        own.append(block)
        grads.append(block)
        at = 2 * p * edge
        after = pltpu.roll(side, (-(at + edge)) % LANES, 1)
        ahead = pltpu.roll(side, (LANES - edge - at) % LANES, 1)
        edges.append(jnp.where(spot < edge, after, ahead).astype(jnp.bfloat16))

    put_grad(grad, jnp.concatenate(grads, axis=1), table)

    def put(q, block):
        haloed[:, q * LANES : (q + 1) * LANES] = block

    if groups > 1:
        fetch(weight, base, buffer, sems, 1).start()
    spread_blocks(blocks, utterances, 1, own, edges, put)
    total = whole if last else next_up
    for g in range(groups):
        fetch(weight, base, buffer, sems, g).wait()
        if g + 2 < groups:
            fetch(weight, base, buffer, sems, g + 2).start()
        lhs = jnp.concatenate([buffer[g, k] for k in range(GROUP)], axis=1)
        starts = [(taps - 1 - g * GROUP - k) * LANES for k in range(GROUP)]
        rhs = jnp.concatenate([haloed[:, at : at + rows] for at in starts], axis=0)
        product = jnp.dot(lhs, rhs, preferred_element_type=jnp.float32)
        total[...] = product if g == 0 else total[...] + product
    if last:
        for p in range(phases):
            give(staged, slice(None), total[:, p * LANES : (p + 1) * LANES].T)
            for u in range(utterances):
                mask = span_of(info, utterances, phases, p, u, (LANES // utterances, cin))
                give(laid, frames_of(utterances, phases, p, u), take(staged, rows_of(utterances, 0, u)) * mask)
        unlay(laid, next_up)
        return
    gains = jnp.zeros((cin, LANES), jnp.float32)
    biases = jnp.zeros((cin, LANES), jnp.float32)
    ends = jnp.zeros((cin, LANES), jnp.float32)
    spot = lax.broadcasted_iota(jnp.int32, (cin, LANES), 1)
    for p in range(phases):
        cut = slice(p * LANES, (p + 1) * LANES)
        mask = valid_of(info, utterances, phases, p, 0, (1, LANES), 1)
        value = before[:, cut].astype(jnp.float32)
        block = next_up[:, cut] * mask * silu_slope(value * column(3) + column(4))
        next_up[:, cut] = block
        gains += block * (value * column(5) + column(6))
        biases += block
        at = 2 * p * edge
        rolled = pltpu.roll(block, (at + edge) % LANES, 1)
        ends = jnp.where((spot >= at) & (spot < at + 2 * edge), rolled, ends)
    ends = ends.T
    for p in range(phases):
        at = 2 * p * edge
        low_out[p] = ends[at : at + edge, :]
        high_out[p] = ends[at + edge : at + 2 * edge, :]
    gains = jnp.sum(gains.T, axis=0, keepdims=True)
    biases = jnp.sum(biases.T, axis=0, keepdims=True)
    put_sums(sums, [gains, biases])


def backward_conv(
    utterances, info, up, linear, low_up, high_up, low_lin, high_lin, came, came_up, gain, before, came_before,
    gain_before, bias_before, weight, layer, copies, split, table,
):
    _, taps, cin, cout = weight.shape
    rows = up.shape[1]
    phases, blocks, edge = plan(utterances, rows, taps)
    groups = taps // GROUP
    last = before is None
    if last:
        before = jnp.zeros((16, LANES), jnp.bfloat16)
        came_before = jnp.zeros((1, 8, LANES), jnp.float32)
        gain_before = bias_before = jnp.zeros((1, LANES), jnp.float32)
    shape = jax.ShapeDtypeStruct
    cfg = (utterances, phases, blocks, edge, taps, layer * groups, last, table)
    return pl.pallas_call(
        functools.partial(backward_kernel, cfg),
        name="backward_conv",
        out_shape=(
            shape(split + (rows,), jnp.bfloat16),
            shape((rows, cin) if last else (cin, rows), jnp.float32),
            shape((copies, pieces_of(2 * cin), LANES), jnp.float32),
            shape((phases, edge, cin), jnp.float32),
            shape((phases, edge, cin), jnp.float32),
            shape((1, 2 * cout), jnp.float32),
        ),
        in_specs=[SMEM] + [VMEM] * 13 + [ANY],
        out_specs=(VMEM,) * 6,
        scratch_shapes=[
            pltpu.VMEM((groups, GROUP, cin, cout), jnp.bfloat16),
            pltpu.VMEM((cout, len(blocks) * LANES), jnp.bfloat16),
            pltpu.SemaphoreType.DMA((groups,)),
            pltpu.VMEM((cin // LANES, LANES, LANES), jnp.float32),
            pltpu.VMEM((cin, rows) if last else (8, LANES), jnp.float32),
            pltpu.VMEM((cin // LANES, rows, LANES) if last else (1, 8, LANES), jnp.float32),
        ],
        compiler_params=PARAMS,
        cost_estimate=pl.CostEstimate(
            flops=2 * taps * rows * cin * cout, bytes_accessed=2 * taps * cin * cout, transcendentals=0
        ),
    )(
        info, up, linear, low_up, high_up, low_lin, high_lin, came, came_up, gain, before, came_before,
        gain_before, bias_before, weight.reshape(-1, GROUP, cin, cout),
    )


def weight_kernel(cfg, info, hidden_all, *refs):
    utterances, phases, blocks, taps, batch, first, parts = cfg
    pieces, (out, hidden, grad, haloed, total, sems) = refs[:parts], refs[parts:]
    inner, width, cin, rows = hidden.shape
    cout = grad.shape[2]
    across = width // parts

    def copies_of(b):
        for p, piece in enumerate(pieces):
            for x in range(across):
                at = (p * inner + b) * across + x
                yield pltpu.make_async_copy(piece.at[b * across + x], grad.at[at], sems.at[at])
        source = hidden_all.at[b, :, pl.ds(first, cin), :]
        yield pltpu.make_async_copy(source, hidden.at[b], sems.at[width * inner + b])

    def start(b, carry):
        for copy in copies_of(b):
            copy.start()
        return carry

    lax.fori_loop(0, inner, start, 0)
    total[...] = jnp.zeros_like(total)
    zero = jnp.zeros((cin, LANES), hidden.dtype)
    spot = lax.broadcasted_iota(jnp.int32, (cin, LANES), 1)

    def unit(b, carry):
        for copy in copies_of(b):
            copy.wait()
        for t in range(width):
            for q, (phase, move) in enumerate(blocks):
                cut = slice(phase * LANES, (phase + 1) * LANES)
                block = hidden[b, t, :, cut]
                if move:
                    if move > 0:
                        other = hidden[b, t + 1, :, cut] if t + 1 < width else zero
                        outside = spot < move * utterances
                    else:
                        other = hidden[b, t - 1, :, cut] if t > 0 else zero
                        outside = spot >= LANES + move * utterances
                    block = pltpu.roll(jnp.where(outside, other, block), (-move * utterances) % LANES, 1)
                haloed[t, :, q * LANES : (q + 1) * LANES] = block
        lhs = jnp.concatenate(
            [grad[(p * inner + b) * across + x] for p in range(parts) for x in range(across)], axis=1
        )

        places = [x * parts + jnp.bitwise_xor(info[0], p) for p in range(parts) for x in range(across)]
        for g in range(taps // batch):
            rhs = jnp.concatenate(
                [
                    jnp.concatenate([haloed[place, :, k * LANES : k * LANES + rows] for place in places], axis=1)
                    for k in range(g * batch, (g + 1) * batch)
                ],
                axis=0,
            )
            total[g] += lax.dot_general(
                lhs, rhs, (((1,), (1,)), ((), ())), preferred_element_type=jnp.float32
            )
        return carry

    lax.fori_loop(0, inner, unit, 0)
    outer, _, cols, _ = out.shape
    for z in range(outer):
        out[z] = total[:, z * cols : (z + 1) * cols, :].astype(jnp.bfloat16)


def weight_grad(utterances, taps, order, hidden, first, cin, grad, outer):
    inner, width, _, rows = hidden.shape
    cout = grad[0].shape[1]
    phases, blocks, _ = plan(utterances, rows, taps)
    batch = 7
    cfg = (utterances, phases, blocks, taps, batch, first, len(grad))
    return pl.pallas_call(
        functools.partial(weight_kernel, cfg),
        name="weight_grad",
        out_shape=jax.ShapeDtypeStruct((outer, taps // batch, cout // outer, batch * cin), jnp.bfloat16),
        in_specs=[SMEM] + [ANY] * (1 + len(grad)),
        out_specs=VMEM,
        scratch_shapes=[
            pltpu.VMEM((inner, width, cin, rows), jnp.bfloat16),
            pltpu.VMEM((width * inner, cout, rows), jnp.bfloat16),
            pltpu.VMEM((width, cin, len(blocks) * LANES), jnp.bfloat16),
            pltpu.VMEM((taps // batch, cout, batch * cin), jnp.float32),
            pltpu.SemaphoreType.DMA((inner + width * inner,)),
        ],
        compiler_params=PARAMS,
        cost_estimate=pl.CostEstimate(
            flops=2 * taps * inner * width * rows * cin * cout,
            bytes_accessed=2 * inner * width * rows * (cin + cout),
            transcendentals=0,
        ),
    )(order, hidden, *grad)


def branch_terms(first, second, counted, channels):
    at = 2 * channels + LANES
    average = flat_sums(first[...])[:, at : at + channels] / counted
    square = flat_sums(second[...])[:, at : at + channels] / counted
    return average, lax.rsqrt(square - average * average + EPSILON)


def middle_kernel(
    cfg, info, linear, came, first, second, branch, cotangent, gain, bias, branch_gain, branch_bias, result, up, turned, sums,
    low_out, high_out, staged, linear_laid, branch_laid, cotangent_laid, result_laid, up_laid,
):
    utterances, phases, edge = cfg
    channels = linear.shape[1]
    average, inv, counted = norm_terms(came[...], channels)
    branch_average, branch_inv = branch_terms(first, second, counted, channels)
    zero = jnp.zeros((1, channels), jnp.float32)
    gain_sum, bias_sum, branch_sum = zero, zero, zero
    lay(linear, linear_laid)
    lay(branch, branch_laid)
    lay(cotangent, cotangent_laid)
    shape = (LANES // utterances, 1)
    for p in range(phases):
        for u in range(utterances):
            here = frames_of(utterances, phases, p, u)
            frame = info[utterances] + lax.broadcasted_iota(jnp.int32, shape, 0) * phases + p
            mask = (frame < info[u]).astype(jnp.float32)
            scaled = (take(linear_laid, rows_of(utterances, p * LANES, u)) - average) * inv
            branch_scaled = (take(branch_laid, here) - branch_average) * branch_inv
            joined = scaled * gain[...] + bias[...] + (branch_scaled * branch_gain[...] + branch_bias[...])
            logistic = jax.nn.sigmoid(joined)
            give(result_laid, here, joined * logistic * mask)
            grad = take(cotangent_laid, here) * mask * (logistic * (1.0 + joined * (1.0 - logistic)))
            give(up_laid, here, grad)
            give(staged, rows_of(utterances, 0, u), grad)
            gain_sum += jnp.sum(grad * scaled, axis=0, keepdims=True)
            bias_sum += jnp.sum(grad, axis=0, keepdims=True)
            branch_sum += jnp.sum(grad * branch_scaled, axis=0, keepdims=True)
        block = take(staged, slice(None))
        turned[:, p * LANES : (p + 1) * LANES] = block.T
        low_out[p] = block[LANES - edge :, :]
        high_out[p] = block[:edge, :]
    unlay(result_laid, result)
    unlay(up_laid, up)
    put_sums(sums, [gain_sum, bias_sum, branch_sum])


def middle(utterances, info, linear, came, first, second, branch, cotangent, terms, edge, copies):
    rows, channels = linear.shape
    phases = rows // LANES
    shape = jax.ShapeDtypeStruct
    return pl.pallas_call(
        functools.partial(middle_kernel, (utterances, phases, edge)),
        name="middle",
        out_shape=(
            shape((rows, channels), jnp.float32),
            shape((rows, channels), jnp.float32),
            shape((channels, rows), jnp.float32),
            shape((copies, pieces_of(3 * channels), LANES), jnp.float32),
            shape((phases, edge, channels), jnp.float32),
            shape((phases, edge, channels), jnp.float32),
        ),
        in_specs=[SMEM] + [VMEM] * 10,
        out_specs=(VMEM,) * 6,
        scratch_shapes=[pltpu.VMEM((channels // LANES, LANES, LANES), jnp.float32)]
        + [pltpu.VMEM((channels // LANES, rows, LANES), jnp.float32)] * 5,
        compiler_params=PARAMS,
        cost_estimate=pl.CostEstimate(
            flops=40 * rows * channels, bytes_accessed=24 * rows * channels, transcendentals=rows * channels
        ),
    )(info, linear, came, first, second, branch, cotangent, *terms)


def residual_kernel(cfg, info, dense, branch, up, first, second, came_up, gain, grad, product):
    utterances, parts = cfg
    rows, channels = branch.shape
    total = flat_sums(came_up[...])
    counted = flat_sums(first[...])[:, 2 * channels : 2 * channels + 1]
    average, inv = branch_terms(first, second, counted, channels)
    keep_up = gain[...] * inv
    keep_branch = -keep_up * inv * total[:, 2 * channels : 3 * channels] / counted
    rest = -keep_up * total[:, channels : 2 * channels] / counted - keep_branch * average
    count = rows // utterances
    frame = info[utterances] + lax.broadcasted_iota(jnp.int32, (count, 1), 0)
    mask = jnp.concatenate([(frame < info[u]).astype(jnp.float32) for u in range(utterances)], axis=0)
    value = (mask * (up[...] * keep_up + branch[...] * keep_branch + rest)).astype(jnp.bfloat16)
    grad[...] = value
    turned = value.T
    size = dense.shape[1] // parts
    if size % LANES == 0:
        for t in range(parts):
            low = (dense[:, t * size : (t + 1) * size] * mask).astype(jnp.bfloat16)
            product[t] = jnp.dot(turned, low, preferred_element_type=jnp.float32).astype(jnp.bfloat16)
    else:
        low = (dense[...] * mask).astype(jnp.bfloat16)
        every_part = jnp.dot(turned, low, preferred_element_type=jnp.float32).astype(jnp.bfloat16)
        for t in range(parts):
            product[t] = every_part[:, t * size : (t + 1) * size]


def residual(utterances, info, dense, branch, up, first, second, came_up, gain, parts):
    rows, channels = branch.shape
    deep = dense.shape[1]
    shape = jax.ShapeDtypeStruct
    return pl.pallas_call(
        functools.partial(residual_kernel, (utterances, parts)),
        name="residual",
        out_shape=(
            shape((rows, channels), jnp.bfloat16),
            shape((parts, channels, deep // parts), jnp.bfloat16),
        ),
        in_specs=[SMEM] + [VMEM] * 7,
        out_specs=(VMEM,) * 2,
        compiler_params=PARAMS,
        cost_estimate=pl.CostEstimate(
            flops=2 * rows * channels * deep, bytes_accessed=4 * rows * deep, transcendentals=0
        ),
    )(info, dense, branch, up, first, second, came_up, gain)


def finish_kernel(cfg, *refs):
    taps, terms, turned = cfg
    parts, out = refs[:terms], refs[-1]
    groups = parts[0].shape[0]
    batch = taps // groups
    for g in range(groups):
        block = parts[0][g].astype(jnp.float32)
        for part in parts[1:]:
            block += part[g].astype(jnp.float32)
        size = block.shape[1] // batch
        if turned:
            for k in range(batch):
                out[g * batch + k] = block[:, k * size : (k + 1) * size]
        else:
            out[g * batch : (g + 1) * batch] = block.T.reshape(batch, size, block.shape[0])


def finish(taps, parts, layer=0, layers=1, buffer=None, turned=False):
    groups, cols, long = parts[0].shape
    cin = long * groups // taps
    block = (taps, cols, cin) if turned else (taps, cin, cols)
    extra = [] if buffer is None else [buffer]
    return pl.pallas_call(
        functools.partial(finish_kernel, (taps, len(parts), turned)),
        name="finish",
        grid=(1,),
        out_shape=jax.ShapeDtypeStruct((layers,) + block, jnp.float32),
        in_specs=[VMEM] * len(parts) + [ANY] * len(extra),
        out_specs=pl.BlockSpec((None,) + block, lambda i: (layer, 0, 0, 0)),
        input_output_aliases={len(parts): 0} if extra else {},
        compiler_params=PARAMS,
    )(*parts, *extra)


def span_keep(span_cols, positions):
    inside = (positions[None, :] >= span_cols[:, 0:1]) & (
        positions[None, :] < span_cols[:, 0:1] + span_cols[:, 1:2]
    )
    return 1.0 - inside.astype(jnp.float32)


def edge_rows(frames, phases):
    utterances, count, channels = frames.shape
    cut = frames.reshape(utterances, count // phases, phases, channels).transpose(2, 1, 0, 3)
    return cut.reshape(phases, utterances * count // phases, channels)


def swap_edges(low_out, high_out):
    count = lax.axis_size(TIME)
    low = lax.ppermute(low_out, TIME, [(i, i + 1) for i in range(count - 1)])
    high = lax.ppermute(high_out, TIME, [(i + 1, i) for i in range(count - 1)])
    return low, high


def every(copies):
    return lax.all_to_all(copies, ALL, split_axis=0, concat_axis=0, tiled=True)


def body(
    features,
    dense_input,
    lengths,
    time_span,
    freq_span,
    w_first,
    w_rest,
    w_res,
    norm_gains,
    norm_biases,
    cotangent,
):
    utterances, frames_here, in_channels = features.shape
    high_z, low_z, inner, across, cores = (lax.axis_size(name) for name in ALL)
    outer = high_z * low_z
    width = across * cores
    copies = outer * inner * width
    taps, _, channels = w_first.shape
    blocks = 1 + w_rest.shape[0]
    rows = utterances * frames_here
    phases, _, edge = plan(utterances, rows, taps)
    cols = channels // (outer * inner)
    late = 0
    whole_table = [[z * inner + y for z in range(outer)] for y in range(inner)]
    half_table = [
        [(h * low_z + l) * inner + y for h in range(high_z)] for l in range(low_z) for y in range(inner)
    ]
    offset = lax.axis_index(TIME) * frames_here
    spans = jnp.concatenate([time_span, freq_span], axis=1).reshape(-1)
    info = jnp.concatenate([lengths, jnp.stack([offset, 0]).astype(jnp.int32), spans])
    frames = offset + jnp.arange(frames_here, dtype=jnp.int32)
    valid = (frames[None, :] < lengths[:, None]).astype(jnp.float32)[:, :, None]
    layers = [(w_first[None], 0)] + [(w_rest, s) for s in range(blocks - 1)]
    gains = [norm_gains[s : s + 1] for s in range(blocks + 1)]
    biases = [norm_biases[s : s + 1] for s in range(blocks + 1)]

    def masked_edge(first, count):
        at = frames[first : first + count]
        keep = (at[None, :] < lengths[:, None]).astype(jnp.float32)[:, :, None]
        keep *= span_keep(time_span, at)[:, :, None]
        keep *= span_keep(freq_span, jnp.arange(in_channels, dtype=jnp.int32))[:, None, :]
        cut = (features[:, first : first + count] * keep).astype(jnp.bfloat16)
        return edge_rows(cut.astype(jnp.float32), phases)

    def spread_hidden(turned):
        cut = turned.reshape(width, turned.shape[0] // width, rows)
        return lax.all_to_all(cut, TIME, split_axis=0, concat_axis=0, tiled=True)

    def gather_hidden(near, s):
        return lax.all_gather(near, "y" if s >= late else ("zl", "y"))

    def plan_grad(s):
        table, axes = (whole_table, ("y",)) if s >= late else (half_table, ("zl", "y"))
        split = (len(table), across, len(table[0]), cols) if cols % 16 == 0 else (channels,)
        return table, split, axes + ("x",)

    def spread_grad(grad, s):
        table, _, axes = plan_grad(s)
        if grad.ndim == 2:
            cut = grad.reshape(outer * inner, cols, rows)[jnp.array(table)][:, None]
            grad = jnp.broadcast_to(cut, (len(table), across) + cut.shape[2:])
        grad = grad.reshape(len(table) * across, -1, rows)
        return lax.all_to_all(grad, axes, split_axis=0, concat_axis=0, tiled=True)

    def other_core(near):
        return lax.ppermute(near, "core", [(0, 1), (1, 0)]) if cores == 2 else None

    def grad_of_weights(hidden, near, far, s):
        pieces, order = [near], jnp.zeros((1,), jnp.int32)
        if far is not None:
            pieces.append(far)
            order = lax.axis_index("core").astype(jnp.int32)[None]
        places = outer if s >= late else high_z
        return weight_grad(utterances, taps, order, hidden, 0, hidden.shape[2], pieces, places)

    def sum_over_z_by_pairs(part):
        if (high_z, low_z) != (2, 2):
            return sum_over_z(part, 0)
        me = 2 * lax.axis_index("zh") + lax.axis_index("zl")

        def block(bits):
            return lax.dynamic_index_in_dim(part, jnp.bitwise_xor(me, bits), 0, keepdims=False)

        across = lax.ppermute(block(3), "zl", [(0, 1), (1, 0)])
        beside = lax.ppermute(block(1), "zl", [(0, 1), (1, 0)])
        both = (block(2).astype(jnp.float32) + across.astype(jnp.float32)).astype(jnp.bfloat16)
        return [block(0), beside, lax.ppermute(both, "zh", [(0, 1), (1, 0)])]

    def sum_over_z(part, s):
        if s >= late:
            return [lax.psum_scatter(part, DEPTH, scatter_dimension=0, tiled=True)[0]]
        if high_z != 2:
            return [lax.psum_scatter(part, "zh", scatter_dimension=0, tiled=True)[0]]
        me = lax.axis_index("zh")
        away = lax.dynamic_index_in_dim(part, 1 - me, 0, keepdims=False)
        came = lax.ppermute(away, "zh", [(0, 1), (1, 0)])
        own = lax.dynamic_index_in_dim(part, me, 0, keepdims=False)
        return [own, came]

    reach = edge * phases // utterances
    low, high = swap_edges(masked_edge(frames_here - reach, reach), masked_edge(0, reach))
    source = features.reshape(rows, in_channels)
    dense_low = (dense_input * valid).astype(jnp.bfloat16)
    branch = jnp.einsum("utd,dc->utc", dense_low, w_res, preferred_element_type=jnp.float32)
    branch_sums = {
        blocks - 3: jnp.sum(branch * valid, axis=(0, 1))[None],
        blocks - 2: jnp.sum(branch * branch * valid, axis=(0, 1))[None],
    }
    came_all, hidden_all, turned_all, edges_all = [], [], [], []
    came = None
    near = None
    for s in range(blocks):
        weight, layer = layers[s]
        more = branch_sums.get(s)
        source, sums, low_out, high_out, flat, turned = forward_conv(
            utterances, info, source, low, high, came, gains[s - 1], biases[s - 1], weight, layer, copies, more
        )
        if near is not None:
            done = hidden_all[: max(s - 2, 0)]
            sums, near, done = lax.optimization_barrier((sums, near, done))
            hidden_all[: len(done)] = done
            hidden_all.append(gather_hidden(near, s - 1))
        low, high = swap_edges(low_out, high_out)
        came = every(sums)
        flat, came, low, high = lax.optimization_barrier((flat, came, low, high))
        if s + 1 < blocks:
            near = spread_hidden(flat)
        came_all.append(came)
        turned_all.append(turned)
        edges_all.append((low, high))

    result, upstream, up, sums, low_out, high_out = middle(
        utterances,
        info,
        source,
        came,
        came_all[blocks - 3],
        came_all[blocks - 2],
        branch.reshape(rows, channels),
        cotangent.reshape(rows, channels),
        (gains[blocks - 1], biases[blocks - 1], gains[blocks], biases[blocks]),
        edge,
        copies,
    )
    done = hidden_all[: blocks - 2]
    sums, done = lax.optimization_barrier((sums, done))
    hidden_all[: len(done)] = done
    low_up, high_up = swap_edges(low_out, high_out)
    came_up = every(sums)
    flat, came_up, low_up, high_up = lax.optimization_barrier((flat, came_up, low_up, high_up))
    hidden_near = spread_hidden(flat)

    def row_of(terms):
        return jnp.sum(terms, axis=0).reshape(1, -1)

    total = row_of(came_up)
    gain_grads, bias_grads = [None] * (blocks + 1), [None] * (blocks + 1)
    gain_grads[blocks], bias_grads[blocks] = total[:, 2 * channels : 3 * channels], total[:, channels : 2 * channels]
    branch_grad, grad_res = residual(
        utterances,
        info,
        dense_input.reshape(rows, -1),
        branch.reshape(rows, channels),
        upstream,
        came_all[blocks - 3],
        came_all[blocks - 2],
        came_up,
        gains[blocks],
        width,
    )
    branch_grad = branch_grad.reshape(branch.shape)
    up, hidden_near, grad_res = lax.optimization_barrier((up, hidden_near, grad_res))
    hidden_all.append(gather_hidden(hidden_near, blocks - 1))

    parts = [None] * blocks
    near = None
    for s in range(blocks - 1, -1, -1):
        weight, layer = layers[s]
        if s == 0 and near is not None:
            up, near = lax.optimization_barrier((up, near))
        if s + 2 < blocks:
            up, parts[s + 2] = lax.optimization_barrier((up, parts[s + 2]))
            parts[s + 2] = sum_over_z(parts[s + 2], s + 2)
        before = (None,) * 4
        table, split, _ = plan_grad(s)
        if s > 0:
            before = (turned_all[s - 1], came_all[s - 1], gains[s - 1], biases[s - 1])
        grad, up, sums, low_out, high_out, total = backward_conv(
            utterances, info, up, turned_all[s], low_up, high_up, *edges_all[s], came_all[s], came_up,
            gains[s], *before, weight, layer, copies, split, table,
        )
        gain_grads[s], bias_grads[s] = total[:, :channels], total[:, channels:]
        if near is not None and s > 0:
            sums, near = lax.optimization_barrier((sums, near))
            if s + 2 == blocks:
                near, grad_res, hidden_all = lax.optimization_barrier((near, grad_res, hidden_all))
                grad_res = lax.psum_scatter(grad_res, TIME, scatter_dimension=0, tiled=True)[0]
        elif near is not None:
            up, near = lax.optimization_barrier((up, near))
        if s > 0:
            low_up, high_up = swap_edges(low_out, high_out)
            came_up = every(sums)
            far = None if near is None else other_core(near)
            grad, came_up, low_up, high_up, near, far = lax.optimization_barrier(
                (grad, came_up, low_up, high_up, near, far)
            )
        elif near is not None:
            far = other_core(near)
        if near is not None:
            parts[s + 1] = grad_of_weights(hidden_all[s + 1], near, far, s + 1)
        near = spread_grad(grad, s)
    grad_dense = (
        jnp.einsum("utc,dc->utd", branch_grad, w_res, preferred_element_type=jnp.float32) * valid
    )
    near, parts[1], grad_res, grad_dense = lax.optimization_barrier((near, parts[1], grad_res, grad_dense))
    grad_res = grad_res.reshape(high_z * low_z * inner, cols, -1)
    grad_res = lax.all_to_all(grad_res, BATCH, split_axis=0, concat_axis=0, tiled=True)
    grad_res = jnp.sum(grad_res.astype(jnp.float32), axis=0)
    parts[0] = grad_of_weights(hidden_all[0], near, other_core(near), 0)
    parts[1] = sum_over_z(parts[1], 1)
    parts[0] = sum_over_z_by_pairs(parts[0])
    turned = in_channels // width % LANES == 0
    grad_first = finish(taps, parts[0], turned=turned)[0]
    grad_first = grad_first.transpose(0, 2, 1) if turned else grad_first
    grad_rest = None
    for s in range(blocks - 1, 0, -1):
        grad_rest = finish(taps, parts[s], s - 1, blocks - 1, grad_rest)
    grad_features = up.reshape(features.shape)

    return (
        result.reshape(cotangent.shape),
        grad_features,
        grad_dense,
        grad_first,
        grad_rest,
        grad_res.T,
        jnp.concatenate(gain_grads, axis=0),
        jnp.concatenate(bias_grads, axis=0),
    )


def solution(mesh):
    batch, tm = mesh.shape["batch"], mesh.shape["tm"]
    side = math.isqrt(batch // 2)
    side = side if batch % max(side, 1) == 0 else 1
    deep = batch // side
    low = 2 if deep % 2 == 0 else 1
    cores = 2 if tm % 2 == 0 else 1
    cut = Mesh(mesh.devices.reshape(deep // low, low, side, tm // cores, cores), ALL)
    rows = P(BATCH, TIME, None)
    placed = (rows, rows, P(BATCH), P(BATCH, None), P(BATCH, None))
    placed += (P(), P(), P(), P(), P(), rows)
    return jax.shard_map(
        body,
        mesh=cut,
        in_specs=placed,
        out_specs=(
            rows,
            rows,
            rows,
            P(None, TIME, BATCH),
            P(None, None, TIME, BATCH),
            P(TIME, BATCH),
            P(),
            P(),
        ),
        check_vma=False,
    )
```

time: 2520 us -> 608 us (0.24)
  waiting for transfers between devices: 1380 us -> 144 us
  blocking collectives: 419 us -> 0 us
  matrix products: 288 us -> 11.5 us
  Pallas kernels: 0 us -> 264 us
  other arithmetic: 242 us -> 8.82 us
  local copies, waits for them, and re-layouts: 131 us -> 15.4 us
  starting transfers between devices: 39.3 us -> 138 us
    reduce_scatter x6 -> x5, waiting for transfers between devices: 1250 us -> 0.03 us  [the longest x1 0.02 us: body(): lax.psum_scatter(grad_res, TIME, scatter_dimension=0, tiled=True)[0]]
    psum x10 -> x0, blocking collectives: 419 us -> none  [the longest x5 202 us: reduce_back(): return lax.psum(local_sums, ('batch', 'tm'))]
    dot_general x16 -> x0, matrix products: 276 us -> none  [the longest x5 96.8 us: run(): jnp.einsum('utki,kic->utc', shifted_taps(padded, kernel_len, frames_here,...]
    pallas_call x0 -> x22, Pallas kernels: none -> 264 us  [the longest x5 84.5 us: forward_conv(): pl.pallas_call(kernel, name='forward_conv', out_shape=(shape((rows, cout)...]
    unnamed x195 -> x0, other arithmetic: 183 us -> none
    unnamed x18 -> x10, waiting for transfers between devices: 125 us -> 1.02 us
    unnamed x137 -> x56, local copies, waits for them, and re-layouts: 128 us -> 6.77 us
    all_to_all x0 -> x21, starting transfers between devices: none -> 91.9 us  [the longest x10 43 us: every(): return lax.all_to_all(copies, ALL, split_axis=0, concat_axis=0, tiled=True)]
  transfers between devices with their start and end apart: 32 -> 61, of which waited for: 10 -> 29; matrix products, arithmetic and copies ran while one was open for 15% -> 4% of each run, Pallas kernels for 0% -> 41%
where the time goes in v1:
time: 608 us; the launch traced here: 597 us
  Pallas kernels  264 us (43%)
  waiting for transfers between devices  144 us (24%)
  starting transfers between devices  138 us (23%)
  local copies, waits for them, and re-layouts  15.4 us (3%)
  between operations  15.3 us (3%)
  matrix products  11.5 us (2%)
  other arithmetic  8.82 us (1%)
    pallas_call x5, Pallas kernels, forward_conv(): pl.pallas_call(kernel, name='forward_conv', out_shape=(shape((rows, cout)...  84.5 us
    pallas_call x5, Pallas kernels, backward_conv(): pl.pallas_call(functools.partial(backward_kernel, cfg), name='backward_co...  77 us
    pallas_call x5, Pallas kernels, weight_grad(): pl.pallas_call(functools.partial(weight_kernel, cfg), name='weight_grad',...  76.3 us
    all_to_all x10, waiting for transfers between devices, every(): return lax.all_to_all(copies, ALL, split_axis=0, concat_axis=0, tiled=True)  48.6 us
    all_to_all x10, starting transfers between devices, every(): return lax.all_to_all(copies, ALL, split_axis=0, concat_axis=0, tiled=True)  43 us
    ppermute x1, waiting for transfers between devices, sum_over_z_by_pairs(): across = lax.ppermute(block(3), 'zl', [(0, 1), (1, 0)])  30.5 us
    ppermute x11, starting transfers between devices, swap_edges(): low = lax.ppermute(low_out, TIME, [(i, i + 1) for i in range(count - 1)])  27.1 us
    ppermute x11, waiting for transfers between devices, swap_edges(): high = lax.ppermute(high_out, TIME, [(i + 1, i) for i in range(count - 1)])  24.5 us
  transfers between devices with their start and end apart: 61, of which 29 were waited for; matrix products, arithmetic and copies ran while one was open for 4% of the time, Pallas kernels for 41%

profile of v1, /device:TPU:0, one launch (start us, length us, event | category | flops | bytes accessed | tf_op | source)
XLA Modules:
  0.0 597.0 jit_solution(6749063142244452214)
XLA Ops:
  19.2 14.8 %forward_conv.5 = (f32[512,640]{1,0:T(8,128)}, f32[32,16,128]{2,1,0:T(8,128)}, f32[4,8,640]{2,1,0:T(8,128)}, f32[4,8,640]{2,1,0:T(8,128)}, bf16[512,512]{1,0:T(8,128)(2,1)}, /*index=5*/bf16[640,512]{1,0:T(8,128)(2,1)}) custom-call(s32[12]{0:T(128)} %pad_add_fusion.1.refs_0_.info, f32[512,512]{1,0:T(8,128)} %bitcast.86, ...), custom_call_target="tpu_custom_call" | custom-call | flops 7046430720 | bytes 13762560 | tf_op jit(solution)/shard_map/forward_conv/pallas_call | solution.py:241
  34.0 7.5 %all-to-all-start = ((f32[32,16,128]{2,1,0:T(8,128)}), f32[32,16,128]{2,1,0:T(8,128)S(1)}, u32[]{:S(2)}, u32[]{:S(2)}) async-start(f32[32,16,128]{2,1,0:T(8,128)} %get-tuple-element.166), calls=%async_computation | async-start | bytes 524288 | tf_op jit(solution)/shard_map/all_to_all | solution.py:700
  56.2 17.4 %forward_conv.6 = (f32[512,640]{1,0:T(8,128)}, f32[32,16,128]{2,1,0:T(8,128)}, f32[4,8,640]{2,1,0:T(8,128)}, f32[4,8,640]{2,1,0:T(8,128)}, bf16[640,512]{1,0:T(8,128)(2,1)}, /*index=5*/bf16[640,512]{1,0:T(8,128)(2,1)}) custom-call(s32[12]{0:T(128)} %pad_add_fusion.1.refs_0_.info, f32[512,640]{1,0:T(8,128)} %get-tuple-element.164.refs_1_, ...), custom_call_target="tpu_custom_call" | custom-call | flops 8808038400 | bytes 17203200 | tf_op jit(solution)/shard_map/forward_conv/pallas_call | solution.py:241
  78.4 5.7 all-to-all-start.2
  84.2 5.8 multiply_reduce_fusion
  99.2 17.5 %forward_conv.7 = (f32[512,640]{1,0:T(8,128)}, f32[32,16,128]{2,1,0:T(8,128)}, f32[4,8,640]{2,1,0:T(8,128)}, f32[4,8,640]{2,1,0:T(8,128)}, bf16[640,512]{1,0:T(8,128)(2,1)}, /*index=5*/bf16[640,512]{1,0:T(8,128)(2,1)}) custom-call(s32[12]{0:T(128)} %pad_add_fusion.1.refs_0_.info, f32[512,640]{1,0:T(8,128)} %get-tuple-element.172.source, ...), custom_call_target="tpu_custom_call" | custom-call | flops 8808038400 | bytes 17203200 | tf_op jit(solution)/shard_map/forward_conv/pallas_call | solution.py:241
  135.2 17.5 %forward_conv.8 = (f32[512,640]{1,0:T(8,128)}, f32[32,16,128]{2,1,0:T(8,128)}, f32[4,8,640]{2,1,0:T(8,128)}, f32[4,8,640]{2,1,0:T(8,128)}, bf16[640,512]{1,0:T(8,128)(2,1)}, /*index=5*/bf16[640,512]{1,0:T(8,128)(2,1)}) custom-call(s32[12]{0:T(128)} %pad_add_fusion.1.refs_0_.info, f32[512,640]{1,0:T(8,128)} %get-tuple-element.182.source, ...), custom_call_target="tpu_custom_call" | custom-call | flops 8808038400 | bytes 17203200 | tf_op jit(solution)/shard_map/forward_conv/pallas_call | solution.py:241
  167.1 4.7 all-to-all-start.7
  171.9 17.4 %forward_conv.9 = (f32[512,640]{1,0:T(8,128)}, f32[32,16,128]{2,1,0:T(8,128)}, f32[4,8,640]{2,1,0:T(8,128)}, f32[4,8,640]{2,1,0:T(8,128)}, bf16[640,512]{1,0:T(8,128)(2,1)}, /*index=5*/bf16[640,512]{1,0:T(8,128)(2,1)}) custom-call(s32[12]{0:T(128)} %pad_add_fusion.1.refs_0_.info, f32[512,640]{1,0:T(8,128)} %get-tuple-element.192.refs_1_, ...), custom_call_target="tpu_custom_call" | custom-call | flops 8808038400 | bytes 17203200 | tf_op jit(solution)/shard_map/forward_conv/pallas_call | solution.py:241
  204.3 6.2 %middle.1 = (f32[512,640]{1,0:T(8,128)}, f32[512,640]{1,0:T(8,128)}, f32[640,512]{1,0:T(8,128)}, f32[32,16,128]{2,1,0:T(8,128)}, f32[4,8,640]{2,1,0:T(8,128)}, /*index=5*/f32[4,8,640]{2,1,0:T(8,128)}) custom-call(s32[12]{0:T(128)} %pad_add_fusion.1.refs_0_.info, f32[512,640]{1,0:T(8,128)} %get-tuple-element.203.linear, f32[32,16,128]{2,1,0:T(8,128)} %copy-done.7, ...), custom_call_target="tpu_custom_call" | custom-call | flops 13107200 | bytes 7864320 | tf_op jit(solution)/shard_map/middle/pallas_call | solution.py:576
  229.3 7.6 %residual.1 = (bf16[512,640]{1,0:T(8,128)(2,1)}, bf16[4,640,640]{2,1,0:T(8,128)(2,1)}) custom-call(s32[12]{0:T(128)} %pad_add_fusion.1.refs_0_.info, f32[512,2560]{1,0:T(8,128)} %bitcast.62, f32[512,640]{1,0:T(8,128)} %bitcast.64, f32[512,640]{1,0:T(8,128)} %get-tuple-element.224.up, f32[32,16,128]{2,1,0:T(8,128)} %copy-done.1, f32[32,16,128]{2,1,0:T(8,128)} %copy-done.2, ...), custom_call_target="tpu_custom_call" | custom-call | flops 1677721600 | bytes 5242880 | tf_op jit(solution)/shard_map/residual/pallas_call | solution.py:629
  239.1 15.9 %backward_conv.5 = (bf16[2,2,4,80,512]{4,3,2,1,0:T(8,128)(2,1)}, f32[640,512]{1,0:T(8,128)}, f32[32,16,128]{2,1,0:T(8,128)}, f32[4,8,640]{2,1,0:T(8,128)}, f32[4,8,640]{2,1,0:T(8,128)}, /*index=5*/f32[1,1280]{1,0:T(1,128)}) custom-call(s32[12]{0:T(128)} %pad_add_fusion.1.refs_0_.info, f32[640,512]{1,0:T(8,128)} %get-tuple-element.227.up, ...), custom_call_target="tpu_custom_call" | custom-call | flops 8808038400 | bytes 17203200 | tf_op jit(solution)/shard_map/backward_conv/pallas_call | solution.py:402
  273.6 15.9 %backward_conv.6 = (bf16[2,2,4,80,512]{4,3,2,1,0:T(8,128)(2,1)}, f32[640,512]{1,0:T(8,128)}, f32[32,16,128]{2,1,0:T(8,128)}, f32[4,8,640]{2,1,0:T(8,128)}, f32[4,8,640]{2,1,0:T(8,128)}, /*index=5*/f32[1,1280]{1,0:T(1,128)}) custom-call(s32[12]{0:T(128)} %pad_add_fusion.1.refs_0_.info, f32[640,512]{1,0:T(8,128)} %get-tuple-element.234.up, ...), custom_call_target="tpu_custom_call" | custom-call | flops 8808038400 | bytes 17203200 | tf_op jit(solution)/shard_map/backward_conv/pallas_call | solution.py:402
  289.5 8.3 %all-to-all-done.12.refs_0_ = bf16[4,320,512]{2,1,0:T(8,128)(2,1)} async-done(((bf16[4,320,512]{2,1,0:T(8,128)(2,1)}), bf16[4,320,512]{2,1,0:T(8,128)(2,1)}, u32[]{:S(2)}, u32[]{:S(2)}) %all-to-all-start.12) | async-done | bytes 1310752 | tf_op jit(solution)/shard_map/all_to_all | solution.py:766
  299.4 4.7 all-to-all-start.13
  314.8 15.7 %weight_grad.5 = bf16[4,3,80,1120]{3,2,1,0:T(8,128)(2,1)} custom-call(s32[1]{0:T(128)} %bitcast.20.info, bf16[2,4,160,512]{3,2,1,0:T(8,128)(2,1)} %bitcast.93, bf16[4,320,512]{2,1,0:T(8,128)(2,1)} %all-to-all-done.12.refs_0_, bf16[4,320,512]{2,1,0:T(8,128)(2,1)} %collective-permute-done.18.refs_1_), custom_call_target="tpu_custom_call" | custom-call | flops 8808038400 | bytes 3932160 | tf_op jit(solution)/shard_map/weight_grad/pallas_call | solution.py:504
  330.6 4.8 all-to-all-start.14
  335.4 16.0 %backward_conv.7 = (bf16[2,2,4,80,512]{4,3,2,1,0:T(8,128)(2,1)}, f32[640,512]{1,0:T(8,128)}, f32[32,16,128]{2,1,0:T(8,128)}, f32[4,8,640]{2,1,0:T(8,128)}, f32[4,8,640]{2,1,0:T(8,128)}, /*index=5*/f32[1,1280]{1,0:T(1,128)}) custom-call(s32[12]{0:T(128)} %pad_add_fusion.1.refs_0_.info, f32[640,512]{1,0:T(8,128)} %get-tuple-element.261.up, ...), custom_call_target="tpu_custom_call" | custom-call | flops 8808038400 | bytes 17203200 | tf_op jit(solution)/shard_map/backward_conv/pallas_call | solution.py:402
  353.9 4.6 all-to-all-start.15
  365.4 9.6 %all-to-all-done.15.came_up = f32[32,16,128]{2,1,0:T(8,128)S(1)} async-done(((f32[32,16,128]{2,1,0:T(8,128)}), f32[32,16,128]{2,1,0:T(8,128)S(1)}, u32[]{:S(2)}, u32[]{:S(2)}) %all-to-all-start.15) | async-done | bytes 262176 | tf_op jit(solution)/shard_map/all_to_all | solution.py:700
  375.1 15.8 %weight_grad.6 = bf16[4,3,80,1120]{3,2,1,0:T(8,128)(2,1)} custom-call(s32[1]{0:T(128)} %bitcast.20.info, bf16[2,4,160,512]{3,2,1,0:T(8,128)(2,1)} %bitcast.92, bf16[4,320,512]{2,1,0:T(8,128)(2,1)} %all-to-all-done.14.refs_0_, bf16[4,320,512]{2,1,0:T(8,128)(2,1)} %collective-permute-done.21.refs_1_), custom_call_target="tpu_custom_call" | custom-call | flops 8808038400 | bytes 3932160 | tf_op jit(solution)/shard_map/weight_grad/pallas_call | solution.py:504
  395.4 16.0 %backward_conv.8 = (bf16[2,2,4,80,512]{4,3,2,1,0:T(8,128)(2,1)}, f32[640,512]{1,0:T(8,128)}, f32[32,16,128]{2,1,0:T(8,128)}, f32[4,8,640]{2,1,0:T(8,128)}, f32[4,8,640]{2,1,0:T(8,128)}, /*index=5*/f32[1,1280]{1,0:T(1,128)}) custom-call(s32[12]{0:T(128)} %pad_add_fusion.1.refs_0_.info, f32[640,512]{1,0:T(8,128)} %get-tuple-element.277.up, ...), custom_call_target="tpu_custom_call" | custom-call | flops 8808038400 | bytes 17203200 | tf_op jit(solution)/shard_map/backward_conv/pallas_call | solution.py:402
  422.9 10.1 %all-to-all-done.17.came_up = f32[32,16,128]{2,1,0:T(8,128)S(1)} async-done(((f32[32,16,128]{2,1,0:T(8,128)}), f32[32,16,128]{2,1,0:T(8,128)S(1)}, u32[]{:S(2)}, u32[]{:S(2)}) %all-to-all-start.17) | async-done | bytes 262176 | tf_op jit(solution)/shard_map/all_to_all | solution.py:700
  438.3 15.8 %weight_grad.7 = bf16[4,3,80,1120]{3,2,1,0:T(8,128)(2,1)} custom-call(s32[1]{0:T(128)} %bitcast.20.info, bf16[2,4,160,512]{3,2,1,0:T(8,128)(2,1)} %bitcast.91, bf16[4,320,512]{2,1,0:T(8,128)(2,1)} %all-to-all-done.16.refs_0_, bf16[4,320,512]{2,1,0:T(8,128)(2,1)} %collective-permute-done.24.refs_1_), custom_call_target="tpu_custom_call" | custom-call | flops 8808038400 | bytes 3932160 | tf_op jit(solution)/shard_map/weight_grad/pallas_call | solution.py:504
  455.5 13.2 %backward_conv.9 = (bf16[2,2,4,80,512]{4,3,2,1,0:T(8,128)(2,1)}, f32[512,512]{1,0:T(8,128)}, f32[32,8,128]{2,1,0:T(8,128)}, f32[4,8,512]{2,1,0:T(8,128)}, f32[4,8,512]{2,1,0:T(8,128)}, /*index=5*/f32[1,1280]{1,0:T(1,128)}) custom-call(s32[12]{0:T(128)} %pad_add_fusion.1.refs_0_.info, f32[640,512]{1,0:T(8,128)} %get-tuple-element.295.up, ...), custom_call_target="tpu_custom_call" | custom-call | flops 7046430720 | bytes 13762560 | tf_op jit(solution)/shard_map/backward_conv/pallas_call | solution.py:402
  468.8 4.8 all-to-all-start.19
  473.6 5.7 convolution_multiply_fusion
  479.3 15.7 %weight_grad.8 = bf16[4,3,80,1120]{3,2,1,0:T(8,128)(2,1)} custom-call(s32[1]{0:T(128)} %bitcast.20.info, bf16[2,4,160,512]{3,2,1,0:T(8,128)(2,1)} %bitcast.90, bf16[4,320,512]{2,1,0:T(8,128)(2,1)} %all-to-all-done.18.refs_0_, bf16[4,320,512]{2,1,0:T(8,128)(2,1)} %collective-permute-done.25.refs_1_), custom_call_target="tpu_custom_call" | custom-call | flops 8808038400 | bytes 3932160 | tf_op jit(solution)/shard_map/weight_grad/pallas_call | solution.py:504
  500.5 13.4 %weight_grad.9 = bf16[4,3,80,896]{3,2,1,0:T(8,128)(2,1)} custom-call(s32[1]{0:T(128)} %bitcast.20.info, bf16[2,4,128,512]{3,2,1,0:T(8,128)(2,1)} %bitcast.94, bf16[4,320,512]{2,1,0:T(8,128)(2,1)} %all-to-all-done.19.refs_0_, bf16[4,320,512]{2,1,0:T(8,128)(2,1)} %collective-permute-done.26.refs_1_), custom_call_target="tpu_custom_call" | custom-call | flops 7046430720 | bytes 3670016 | tf_op jit(solution)/shard_map/weight_grad/pallas_call | solution.py:504
  518.3 30.5 %collective-permute-done.28 = bf16[3,80,896]{2,1,0:T(8,128)(2,1)S(1)} collective-permute-done((bf16[3,80,896]{2,1,0:T(8,128)(2,1)S(1)}, bf16[3,80,896]{2,1,0:T(8,128)(2,1)S(1)}, u32[]{:S(2)}, u32[]{:S(2)}) %collective-permute-start.28) | collective-permute-done | bytes 430112 | tf_op jit(solution)/shard_map/ppermute | solution.py:787
  559.6 18.1 %collective-permute-done.27.refs_1_ = bf16[3,80,896]{2,1,0:T(8,128)(2,1)} collective-permute-done((bf16[3,80,896]{2,1,0:T(8,128)(2,1)}, bf16[3,80,896]{2,1,0:T(8,128)(2,1)}, u32[]{:S(2)}, u32[]{:S(2)}) %collective-permute-start.27) | collective-permute-done | bytes 430112 | tf_op jit(solution)/shard_map/ppermute | solution.py:788
  577.6 5.0 collective-permute-done.29.refs_2_
  (214 shorter events, 200.3 us)
Async XLA Ops:
  34.0 18.1 %all-to-all-start = ((f32[32,16,128]{2,1,0:T(8,128)}), f32[32,16,128]{2,1,0:T(8,128)S(1)}, u32[]{:S(2)}, u32[]{:S(2)}) async-start(f32[32,16,128]{2,1,0:T(8,128)} %get-tuple-element.166), calls=%async_computation | async-start | bytes 524288 | tf_op jit(solution)/shard_map/all_to_all | solution.py:700
  52.1 26.4 %all-to-all-start.1 = ((bf16[4,128,512]{2,1,0:T(8,128)(2,1)}), bf16[4,128,512]{2,1,0:T(8,128)(2,1)}, u32[]{:S(2)}, u32[]{:S(2)}) async-start(bf16[4,128,512]{2,1,0:T(8,128)(2,1)} %bitcast.81), calls=%async_computation.1 | async-start | bytes 1048576 | tf_op jit(solution)/shard_map/all_to_all | solution.py:750
  73.6 17.1 %collective-permute-start.4 = (f32[4,8,640]{2,1,0:T(8,128)}, f32[4,8,640]{2,1,0:T(8,128)}, u32[]{:S(2)}, u32[]{:S(2)}) collective-permute-start(f32[4,8,640]{2,1,0:T(8,128)} %get-tuple-element.177), channel_id=1, source_target_pairs={{0,1},{1,2},{2,3},{4,5},{5,6},{6,7},{8,9},{9,10},{10,11},{12,13},{... | collective-permute-start | bytes 245768 | tf_op jit(solution)/shard_map/ppermute | solution.py:694
  78.4 16.3 %all-to-all-start.2 = ((f32[32,16,128]{2,1,0:T(8,128)}), f32[32,16,128]{2,1,0:T(8,128)S(1)}, u32[]{:S(2)}, u32[]{:S(2)}) async-start(f32[32,16,128]{2,1,0:T(8,128)} %get-tuple-element.176), calls=%async_computation.2 | async-start | bytes 524288 | tf_op jit(solution)/shard_map/all_to_all | solution.py:700
  84.1 68.6 %all-gather.11.cloned.1.call-start = ((), (), s32[]{:S(2)}) async-start(), calls=%async_computation.31 | async-start | bytes 1572864 | tf_op jit(solution)/shard_map/all_gather | solution.py:753
  94.7 22.0 %all-to-all-start.3 = ((bf16[4,160,512]{2,1,0:T(8,128)(2,1)}), bf16[4,160,512]{2,1,0:T(8,128)(2,1)}, u32[]{:S(2)}, u32[]{:S(2)}) async-start(bf16[4,160,512]{2,1,0:T(8,128)(2,1)} %bitcast.76), calls=%async_computation.3 | async-start | bytes 1310720 | tf_op jit(solution)/shard_map/all_to_all | solution.py:750
  120.3 69.0 %all-gather.13.cloned.1.call-start = ((), (), s32[]{:S(2)}) async-start(), calls=%async_computation.32 | async-start | bytes 1966080 | tf_op jit(solution)/shard_map/all_gather | solution.py:753
  131.0 21.7 %all-to-all-start.5 = ((bf16[4,160,512]{2,1,0:T(8,128)(2,1)}), bf16[4,160,512]{2,1,0:T(8,128)(2,1)}, u32[]{:S(2)}, u32[]{:S(2)}) async-start(bf16[4,160,512]{2,1,0:T(8,128)(2,1)} %bitcast.75), calls=%async_computation.5 | async-start | bytes 1310720 | tf_op jit(solution)/shard_map/all_to_all | solution.py:750
  156.4 54.0 %all-gather.15.cloned.1.call-start = ((), (), s32[]{:S(2)}) async-start(), calls=%async_computation.33 | async-start | bytes 1966080 | tf_op jit(solution)/shard_map/all_gather | solution.py:753
  167.1 22.2 %all-to-all-start.7 = ((bf16[4,160,512]{2,1,0:T(8,128)(2,1)}), bf16[4,160,512]{2,1,0:T(8,128)(2,1)}, u32[]{:S(2)}, u32[]{:S(2)}) async-start(bf16[4,160,512]{2,1,0:T(8,128)(2,1)} %bitcast.74), calls=%async_computation.7 | async-start | bytes 1310720 | tf_op jit(solution)/shard_map/all_to_all | solution.py:750
  228.8 69.1 %all-gather.17.cloned.1.call-start = ((), (), s32[]{:S(2)}) async-start(), calls=%async_computation.34 | async-start | bytes 1966080 | tf_op jit(solution)/shard_map/all_gather | solution.py:753
  257.6 41.6 %all-gather.19.cloned.1.call-start = ((), (), s32[]{:S(2)}) async-start(), calls=%async_computation.35 | async-start | bytes 1966080 | tf_op jit(solution)/shard_map/all_gather | solution.py:753
  269.0 28.8 %all-to-all-start.12 = ((bf16[4,320,512]{2,1,0:T(8,128)(2,1)}), bf16[4,320,512]{2,1,0:T(8,128)(2,1)}, u32[]{:S(2)}, u32[]{:S(2)}) async-start(bf16[4,320,512]{2,1,0:T(8,128)(2,1)} %bitcast.67), calls=%async_computation.12 | async-start | bytes 2621440 | tf_op jit(solution)/shard_map/all_to_all | solution.py:766
  273.4 221.8 %reduce-scatter.6.cloned.1.call-start = ((), (), s32[]{:S(2)}) async-start(), calls=%async_computation.26 | async-start | bytes 4096000 | tf_op jit(solution)/shard_map/reduce_scatter | solution.py:900
  299.3 15.5 %collective-permute-start.18 = (bf16[4,320,512]{2,1,0:T(8,128)(2,1)}, bf16[4,320,512]{2,1,0:T(8,128)(2,1)}, u32[]{:S(2)}, u32[]{:S(2)}) collective-permute-start(bf16[4,320,512]{2,1,0:T(8,128)(2,1)} %all-to-all-done.12.refs_0_), channel_id=1, source_target_pairs={{0,1},{1,0},{2,3},{3,2},{4,5},{5,4},{6,7},{7,6},{8,9},{9,8},{10,11... | collective-permute-start | bytes 3932168 | tf_op jit(solution)/shard_map/ppermute | solution.py:769
  299.4 15.4 %all-to-all-start.13 = ((f32[32,16,128]{2,1,0:T(8,128)}), f32[32,16,128]{2,1,0:T(8,128)S(1)}, u32[]{:S(2)}, u32[]{:S(2)}) async-start(f32[32,16,128]{2,1,0:T(8,128)} %get-tuple-element.255), calls=%async_computation.13 | async-start | bytes 524288 | tf_op jit(solution)/shard_map/all_to_all | solution.py:700
  304.1 247.1 %reduce-scatter.14.cloned.1.call-start = ((), (), s32[]{:S(2)}) async-start(), calls=%async_computation.30 | async-start | bytes 2764800 | tf_op jit(solution)/shard_map/reduce_scatter | solution.py:794
  330.6 23.3 %all-to-all-start.14 = ((bf16[4,320,512]{2,1,0:T(8,128)(2,1)}), bf16[4,320,512]{2,1,0:T(8,128)(2,1)}, u32[]{:S(2)}, u32[]{:S(2)}) async-start(bf16[4,320,512]{2,1,0:T(8,128)(2,1)} %bitcast.65), calls=%async_computation.14 | async-start | bytes 2621440 | tf_op jit(solution)/shard_map/all_to_all | solution.py:766
  353.9 21.2 %collective-permute-start.21 = (bf16[4,320,512]{2,1,0:T(8,128)(2,1)}, bf16[4,320,512]{2,1,0:T(8,128)(2,1)}, u32[]{:S(2)}, u32[]{:S(2)}) collective-permute-start(bf16[4,320,512]{2,1,0:T(8,128)(2,1)} %all-to-all-done.14.refs_0_), channel_id=1, source_target_pairs={{0,1},{1,0},{2,3},{3,2},{4,5},{5,4},{6,7},{7,6},{8,9},{9,8},{10,11... | collective-permute-start | bytes 3932168 | tf_op jit(solution)/shard_map/ppermute | solution.py:769
  353.9 21.2 %all-to-all-start.15 = ((f32[32,16,128]{2,1,0:T(8,128)}), f32[32,16,128]{2,1,0:T(8,128)S(1)}, u32[]{:S(2)}, u32[]{:S(2)}) async-start(f32[32,16,128]{2,1,0:T(8,128)} %get-tuple-element.271), calls=%async_computation.15 | async-start | bytes 524288 | tf_op jit(solution)/shard_map/all_to_all | solution.py:700
  358.5 196.5 %reduce-scatter.12.cloned.1.call-start = ((), (), s32[]{:S(2)}) async-start(), calls=%async_computation.29 | async-start | bytes 2764800 | tf_op jit(solution)/shard_map/reduce_scatter | solution.py:794
  390.9 21.5 %all-to-all-start.16 = ((bf16[4,320,512]{2,1,0:T(8,128)(2,1)}), bf16[4,320,512]{2,1,0:T(8,128)(2,1)}, u32[]{:S(2)}, u32[]{:S(2)}) async-start(bf16[4,320,512]{2,1,0:T(8,128)(2,1)} %bitcast.66), calls=%async_computation.16 | async-start | bytes 2621440 | tf_op jit(solution)/shard_map/all_to_all | solution.py:766
  412.3 20.6 %collective-permute-start.24 = (bf16[4,320,512]{2,1,0:T(8,128)(2,1)}, bf16[4,320,512]{2,1,0:T(8,128)(2,1)}, u32[]{:S(2)}, u32[]{:S(2)}) collective-permute-start(bf16[4,320,512]{2,1,0:T(8,128)(2,1)} %all-to-all-done.16.refs_0_), channel_id=1, source_target_pairs={{0,1},{1,0},{2,3},{3,2},{4,5},{5,4},{6,7},{7,6},{8,9},{9,8},{10,11... | collective-permute-start | bytes 3932168 | tf_op jit(solution)/shard_map/ppermute | solution.py:769
  412.4 20.6 %all-to-all-start.17 = ((f32[32,16,128]{2,1,0:T(8,128)}), f32[32,16,128]{2,1,0:T(8,128)S(1)}, u32[]{:S(2)}, u32[]{:S(2)}) async-start(f32[32,16,128]{2,1,0:T(8,128)} %get-tuple-element.286), calls=%async_computation.17 | async-start | bytes 524288 | tf_op jit(solution)/shard_map/all_to_all | solution.py:700
  433.7 21.2 %all-to-all-start.18 = ((bf16[4,320,512]{2,1,0:T(8,128)(2,1)}), bf16[4,320,512]{2,1,0:T(8,128)(2,1)}, u32[]{:S(2)}, u32[]{:S(2)}) async-start(bf16[4,320,512]{2,1,0:T(8,128)(2,1)} %bitcast.68), calls=%async_computation.18 | async-start | bytes 2621440 | tf_op jit(solution)/shard_map/all_to_all | solution.py:766
  438.0 146.9 %reduce-scatter.10.cloned.1.call-start = ((), (), s32[]{:S(2)}) async-start(), calls=%async_computation.28 | async-start | bytes 2764800 | tf_op jit(solution)/shard_map/reduce_scatter | solution.py:794
  468.8 26.3 %all-to-all-start.19 = ((bf16[4,320,512]{2,1,0:T(8,128)(2,1)}), bf16[4,320,512]{2,1,0:T(8,128)(2,1)}, u32[]{:S(2)}, u32[]{:S(2)}) async-start(bf16[4,320,512]{2,1,0:T(8,128)(2,1)} %bitcast.69), calls=%async_computation.19 | async-start | bytes 2621440 | tf_op jit(solution)/shard_map/all_to_all | solution.py:766
  473.6 113.9 %reduce-scatter.8.cloned.1.call-start = ((), (), s32[]{:S(2)}) async-start(), calls=%async_computation.27 | async-start | bytes 2764800 | tf_op jit(solution)/shard_map/reduce_scatter | solution.py:794
  496.1 61.5 %all-to-all-start.20 = ((bf16[8,80,640]{2,1,0:T(8,128)(2,1)}), bf16[8,80,640]{2,1,0:T(8,128)(2,1)}, u32[]{:S(2)}, u32[]{:S(2)}) async-start(bf16[8,80,640]{2,1,0:T(8,128)(2,1)} %bitcast.72), calls=%async_computation.25 | async-start | bytes 1638400 | tf_op jit(solution)/shard_map/all_to_all | solution.py:920
  516.2 32.6 %collective-permute-start.28 = (bf16[3,80,896]{2,1,0:T(8,128)(2,1)S(1)}, bf16[3,80,896]{2,1,0:T(8,128)(2,1)S(1)}, u32[]{:S(2)}, u32[]{:S(2)}) collective-permute-start(bf16[3,80,896]{2,1,0:T(8,128)(2,1)S(1)} %get-tuple-element.326), channel_id=1, source_target_pairs={{0,8},{8,0},{1,9},{9,1},{2,10},{10,2},{3,11},{11,3},{4,12},{12,4},... | collective-permute-start | bytes 1290248 | tf_op jit(solution)/shard_map/ppermute | solution.py:787
  518.2 59.4 %collective-permute-start.27 = (bf16[3,80,896]{2,1,0:T(8,128)(2,1)}, bf16[3,80,896]{2,1,0:T(8,128)(2,1)}, u32[]{:S(2)}, u32[]{:S(2)}) collective-permute-start(bf16[3,80,896]{2,1,0:T(8,128)(2,1)} %get-tuple-element.327), channel_id=1, source_target_pairs={{0,8},{8,0},{1,9},{9,1},{2,10},{10,2},{3,11},{11,3},{4,12},{12,4},... | collective-permute-start | bytes 1290248 | tf_op jit(solution)/shard_map/ppermute | solution.py:788
  550.7 31.9 %collective-permute-start.29 = (bf16[3,80,896]{2,1,0:T(8,128)(2,1)}, bf16[3,80,896]{2,1,0:T(8,128)(2,1)}, u32[]{:S(2)}, u32[]{:S(2)}) collective-permute-start(bf16[3,80,896]{2,1,0:T(8,128)(2,1)} %fusion.4), channel_id=1, source_target_pairs={{0,16},{16,0},{1,17},{17,1},{2,18},{18,2},{3,19},{19,3},{4,20},{20... | collective-permute-start | bytes 1290248 | tf_op jit(solution)/shard_map/ppermute | solution.py:790
  (57 other events, 458.3 us)
Sparse Core Ops, SparseCore 0:
  90.8 22.5 all-gather.10
  125.2 26.9 all-gather.12
  160.7 26.9 all-gather.14
  230.8 23.0 all-gather.16
  259.7 39.5 all-gather.18
  302.2 40.3 reduce-scatter.5
  345.0 51.2 reduce-scatter.13
  398.7 49.5 reduce-scatter.11
  455.0 44.5 reduce-scatter.9
  501.9 78.9 reduce-scatter.7

commit v2 on v1

--- a/solution.py
+++ b/solution.py
@@ -451,11 +451,10 @@
         return carry
 
     lax.fori_loop(0, inner, start, 0)
-    total[...] = jnp.zeros_like(total)
     zero = jnp.zeros((cin, LANES), hidden.dtype)
     spot = lax.broadcasted_iota(jnp.int32, (cin, LANES), 1)
 
-    def unit(b, carry):
+    def unit(b):
         for copy in copies_of(b):
             copy.wait()
         for t in range(width):
@@ -484,12 +483,13 @@
                 ],
                 axis=0,
             )
-            total[g] += lax.dot_general(
+            product = lax.dot_general(
                 lhs, rhs, (((1,), (1,)), ((), ())), preferred_element_type=jnp.float32
             )
-        return carry
-
-    lax.fori_loop(0, inner, unit, 0)
+            total[g] = product if b == 0 else total[g] + product
+
+    for b in range(inner):
+        unit(b)
     outer, _, cols, _ = out.shape
     for z in range(outer):
         out[z] = total[:, z * cols : (z + 1) * cols, :].astype(jnp.bfloat16)

time: 608 us -> 608 us (level)
  transfers between devices with their start and end apart: 61 -> 61, of which waited for: 29 -> 29; matrix products, arithmetic and copies ran while one was open for 4% -> 4% of each run, Pallas kernels for 41% -> 42%
where the time goes in v2:
time: 608 us; the launch traced here: 597 us
  Pallas kernels  266 us (44%)
  waiting for transfers between devices  142 us (23%)
  starting transfers between devices  138 us (23%)
  local copies, waits for them, and re-layouts  15.4 us (3%)
  between operations  15.3 us (3%)
  matrix products  11.5 us (2%)
  other arithmetic  8.82 us (1%)
    pallas_call x5, Pallas kernels, forward_conv(): pl.pallas_call(kernel, name='forward_conv', out_shape=(shape((rows, cout)...  84.5 us
    pallas_call x5, Pallas kernels, weight_grad(): pl.pallas_call(functools.partial(weight_kernel, cfg), name='weight_grad',...  78.2 us
    pallas_call x5, Pallas kernels, backward_conv(): pl.pallas_call(functools.partial(backward_kernel, cfg), name='backward_co...  77.1 us
    all_to_all x10, waiting for transfers between devices, every(): return lax.all_to_all(copies, ALL, split_axis=0, concat_axis=0, tiled=True)  47.7 us
    all_to_all x10, starting transfers between devices, every(): return lax.all_to_all(copies, ALL, split_axis=0, concat_axis=0, tiled=True)  43.3 us
    ppermute x1, waiting for transfers between devices, sum_over_z_by_pairs(): across = lax.ppermute(block(3), 'zl', [(0, 1), (1, 0)])  30.3 us
    ppermute x11, starting transfers between devices, swap_edges(): low = lax.ppermute(low_out, TIME, [(i, i + 1) for i in range(count - 1)])  27.1 us
    ppermute x11, waiting for transfers between devices, swap_edges(): high = lax.ppermute(high_out, TIME, [(i + 1, i) for i in range(count - 1)])  24.5 us
  transfers between devices with their start and end apart: 61, of which 29 were waited for; matrix products, arithmetic and copies ran while one was open for 4% of the time, Pallas kernels for 42%

profile of v2, /device:TPU:0, one launch (start us, length us, event | category | flops | bytes accessed | tf_op | source)
XLA Modules:
  0.0 597.1 jit_solution(7009040429866670066)
XLA Ops:
  19.2 14.8 %forward_conv.5 = (f32[512,640]{1,0:T(8,128)}, f32[32,16,128]{2,1,0:T(8,128)}, f32[4,8,640]{2,1,0:T(8,128)}, f32[4,8,640]{2,1,0:T(8,128)}, bf16[512,512]{1,0:T(8,128)(2,1)}, /*index=5*/bf16[640,512]{1,0:T(8,128)(2,1)}) custom-call(s32[12]{0:T(128)} %pad_add_fusion.1.refs_0_.info, f32[512,512]{1,0:T(8,128)} %bitcast.86, ...), custom_call_target="tpu_custom_call" | custom-call | flops 7046430720 | bytes 13762560 | tf_op jit(solution)/shard_map/forward_conv/pallas_call | solution.py:241
  34.0 7.5 %all-to-all-start = ((f32[32,16,128]{2,1,0:T(8,128)}), f32[32,16,128]{2,1,0:T(8,128)S(1)}, u32[]{:S(2)}, u32[]{:S(2)}) async-start(f32[32,16,128]{2,1,0:T(8,128)} %get-tuple-element.166), calls=%async_computation | async-start | bytes 524288 | tf_op jit(solution)/shard_map/all_to_all | solution.py:700
  56.2 17.4 %forward_conv.6 = (f32[512,640]{1,0:T(8,128)}, f32[32,16,128]{2,1,0:T(8,128)}, f32[4,8,640]{2,1,0:T(8,128)}, f32[4,8,640]{2,1,0:T(8,128)}, bf16[640,512]{1,0:T(8,128)(2,1)}, /*index=5*/bf16[640,512]{1,0:T(8,128)(2,1)}) custom-call(s32[12]{0:T(128)} %pad_add_fusion.1.refs_0_.info, f32[512,640]{1,0:T(8,128)} %get-tuple-element.164.refs_1_, ...), custom_call_target="tpu_custom_call" | custom-call | flops 8808038400 | bytes 17203200 | tf_op jit(solution)/shard_map/forward_conv/pallas_call | solution.py:241
  78.4 5.7 all-to-all-start.2
  84.2 5.8 multiply_reduce_fusion
  99.2 17.5 %forward_conv.7 = (f32[512,640]{1,0:T(8,128)}, f32[32,16,128]{2,1,0:T(8,128)}, f32[4,8,640]{2,1,0:T(8,128)}, f32[4,8,640]{2,1,0:T(8,128)}, bf16[640,512]{1,0:T(8,128)(2,1)}, /*index=5*/bf16[640,512]{1,0:T(8,128)(2,1)}) custom-call(s32[12]{0:T(128)} %pad_add_fusion.1.refs_0_.info, f32[512,640]{1,0:T(8,128)} %get-tuple-element.172.source, ...), custom_call_target="tpu_custom_call" | custom-call | flops 8808038400 | bytes 17203200 | tf_op jit(solution)/shard_map/forward_conv/pallas_call | solution.py:241
  135.2 17.5 %forward_conv.8 = (f32[512,640]{1,0:T(8,128)}, f32[32,16,128]{2,1,0:T(8,128)}, f32[4,8,640]{2,1,0:T(8,128)}, f32[4,8,640]{2,1,0:T(8,128)}, bf16[640,512]{1,0:T(8,128)(2,1)}, /*index=5*/bf16[640,512]{1,0:T(8,128)(2,1)}) custom-call(s32[12]{0:T(128)} %pad_add_fusion.1.refs_0_.info, f32[512,640]{1,0:T(8,128)} %get-tuple-element.182.source, ...), custom_call_target="tpu_custom_call" | custom-call | flops 8808038400 | bytes 17203200 | tf_op jit(solution)/shard_map/forward_conv/pallas_call | solution.py:241
  167.1 4.7 all-to-all-start.7
  171.9 17.4 %forward_conv.9 = (f32[512,640]{1,0:T(8,128)}, f32[32,16,128]{2,1,0:T(8,128)}, f32[4,8,640]{2,1,0:T(8,128)}, f32[4,8,640]{2,1,0:T(8,128)}, bf16[640,512]{1,0:T(8,128)(2,1)}, /*index=5*/bf16[640,512]{1,0:T(8,128)(2,1)}) custom-call(s32[12]{0:T(128)} %pad_add_fusion.1.refs_0_.info, f32[512,640]{1,0:T(8,128)} %get-tuple-element.192.refs_1_, ...), custom_call_target="tpu_custom_call" | custom-call | flops 8808038400 | bytes 17203200 | tf_op jit(solution)/shard_map/forward_conv/pallas_call | solution.py:241
  204.3 6.2 %middle.1 = (f32[512,640]{1,0:T(8,128)}, f32[512,640]{1,0:T(8,128)}, f32[640,512]{1,0:T(8,128)}, f32[32,16,128]{2,1,0:T(8,128)}, f32[4,8,640]{2,1,0:T(8,128)}, /*index=5*/f32[4,8,640]{2,1,0:T(8,128)}) custom-call(s32[12]{0:T(128)} %pad_add_fusion.1.refs_0_.info, f32[512,640]{1,0:T(8,128)} %get-tuple-element.203.linear, f32[32,16,128]{2,1,0:T(8,128)} %copy-done.7, ...), custom_call_target="tpu_custom_call" | custom-call | flops 13107200 | bytes 7864320 | tf_op jit(solution)/shard_map/middle/pallas_call | solution.py:576
  229.3 7.6 %residual.1 = (bf16[512,640]{1,0:T(8,128)(2,1)}, bf16[4,640,640]{2,1,0:T(8,128)(2,1)}) custom-call(s32[12]{0:T(128)} %pad_add_fusion.1.refs_0_.info, f32[512,2560]{1,0:T(8,128)} %bitcast.62, f32[512,640]{1,0:T(8,128)} %bitcast.64, f32[512,640]{1,0:T(8,128)} %get-tuple-element.224.up, f32[32,16,128]{2,1,0:T(8,128)} %copy-done.1, f32[32,16,128]{2,1,0:T(8,128)} %copy-done.2, ...), custom_call_target="tpu_custom_call" | custom-call | flops 1677721600 | bytes 5242880 | tf_op jit(solution)/shard_map/residual/pallas_call | solution.py:629
  239.1 15.9 %backward_conv.5 = (bf16[2,2,4,80,512]{4,3,2,1,0:T(8,128)(2,1)}, f32[640,512]{1,0:T(8,128)}, f32[32,16,128]{2,1,0:T(8,128)}, f32[4,8,640]{2,1,0:T(8,128)}, f32[4,8,640]{2,1,0:T(8,128)}, /*index=5*/f32[1,1280]{1,0:T(1,128)}) custom-call(s32[12]{0:T(128)} %pad_add_fusion.1.refs_0_.info, f32[640,512]{1,0:T(8,128)} %get-tuple-element.227.up, ...), custom_call_target="tpu_custom_call" | custom-call | flops 8808038400 | bytes 17203200 | tf_op jit(solution)/shard_map/backward_conv/pallas_call | solution.py:402
  273.6 15.9 %backward_conv.6 = (bf16[2,2,4,80,512]{4,3,2,1,0:T(8,128)(2,1)}, f32[640,512]{1,0:T(8,128)}, f32[32,16,128]{2,1,0:T(8,128)}, f32[4,8,640]{2,1,0:T(8,128)}, f32[4,8,640]{2,1,0:T(8,128)}, /*index=5*/f32[1,1280]{1,0:T(1,128)}) custom-call(s32[12]{0:T(128)} %pad_add_fusion.1.refs_0_.info, f32[640,512]{1,0:T(8,128)} %get-tuple-element.234.up, ...), custom_call_target="tpu_custom_call" | custom-call | flops 8808038400 | bytes 17203200 | tf_op jit(solution)/shard_map/backward_conv/pallas_call | solution.py:402
  289.5 8.3 %all-to-all-done.12.refs_0_ = bf16[4,320,512]{2,1,0:T(8,128)(2,1)} async-done(((bf16[4,320,512]{2,1,0:T(8,128)(2,1)}), bf16[4,320,512]{2,1,0:T(8,128)(2,1)}, u32[]{:S(2)}, u32[]{:S(2)}) %all-to-all-start.12) | async-done | bytes 1310752 | tf_op jit(solution)/shard_map/all_to_all | solution.py:766
  299.4 4.7 all-to-all-start.13
  314.8 16.3 %weight_grad.5 = bf16[4,3,80,1120]{3,2,1,0:T(8,128)(2,1)} custom-call(s32[1]{0:T(128)} %bitcast.20.info, bf16[2,4,160,512]{3,2,1,0:T(8,128)(2,1)} %bitcast.93, bf16[4,320,512]{2,1,0:T(8,128)(2,1)} %all-to-all-done.12.refs_0_, bf16[4,320,512]{2,1,0:T(8,128)(2,1)} %collective-permute-done.18.refs_1_), custom_call_target="tpu_custom_call" | custom-call | flops 8808038400 | bytes 3932160 | tf_op jit(solution)/shard_map/weight_grad/pallas_call | solution.py:504
  331.1 4.8 all-to-all-start.14
  335.9 16.0 %backward_conv.7 = (bf16[2,2,4,80,512]{4,3,2,1,0:T(8,128)(2,1)}, f32[640,512]{1,0:T(8,128)}, f32[32,16,128]{2,1,0:T(8,128)}, f32[4,8,640]{2,1,0:T(8,128)}, f32[4,8,640]{2,1,0:T(8,128)}, /*index=5*/f32[1,1280]{1,0:T(1,128)}) custom-call(s32[12]{0:T(128)} %pad_add_fusion.1.refs_0_.info, f32[640,512]{1,0:T(8,128)} %get-tuple-element.261.up, ...), custom_call_target="tpu_custom_call" | custom-call | flops 8808038400 | bytes 17203200 | tf_op jit(solution)/shard_map/backward_conv/pallas_call | solution.py:402
  353.9 4.7 all-to-all-start.15
  365.5 9.1 %all-to-all-done.15.came_up = f32[32,16,128]{2,1,0:T(8,128)S(1)} async-done(((f32[32,16,128]{2,1,0:T(8,128)}), f32[32,16,128]{2,1,0:T(8,128)S(1)}, u32[]{:S(2)}, u32[]{:S(2)}) %all-to-all-start.15) | async-done | bytes 262176 | tf_op jit(solution)/shard_map/all_to_all | solution.py:700
  374.5 16.3 %weight_grad.6 = bf16[4,3,80,1120]{3,2,1,0:T(8,128)(2,1)} custom-call(s32[1]{0:T(128)} %bitcast.20.info, bf16[2,4,160,512]{3,2,1,0:T(8,128)(2,1)} %bitcast.92, bf16[4,320,512]{2,1,0:T(8,128)(2,1)} %all-to-all-done.14.refs_0_, bf16[4,320,512]{2,1,0:T(8,128)(2,1)} %collective-permute-done.21.refs_1_), custom_call_target="tpu_custom_call" | custom-call | flops 8808038400 | bytes 3932160 | tf_op jit(solution)/shard_map/weight_grad/pallas_call | solution.py:504
  390.9 4.6 all-to-all-start.16
  395.5 15.9 %backward_conv.8 = (bf16[2,2,4,80,512]{4,3,2,1,0:T(8,128)(2,1)}, f32[640,512]{1,0:T(8,128)}, f32[32,16,128]{2,1,0:T(8,128)}, f32[4,8,640]{2,1,0:T(8,128)}, f32[4,8,640]{2,1,0:T(8,128)}, /*index=5*/f32[1,1280]{1,0:T(1,128)}) custom-call(s32[12]{0:T(128)} %pad_add_fusion.1.refs_0_.info, f32[640,512]{1,0:T(8,128)} %get-tuple-element.277.up, ...), custom_call_target="tpu_custom_call" | custom-call | flops 8808038400 | bytes 17203200 | tf_op jit(solution)/shard_map/backward_conv/pallas_call | solution.py:402
  423.2 9.8 %all-to-all-done.17.came_up = f32[32,16,128]{2,1,0:T(8,128)S(1)} async-done(((f32[32,16,128]{2,1,0:T(8,128)}), f32[32,16,128]{2,1,0:T(8,128)S(1)}, u32[]{:S(2)}, u32[]{:S(2)}) %all-to-all-start.17) | async-done | bytes 262176 | tf_op jit(solution)/shard_map/all_to_all | solution.py:700
  438.1 16.3 %weight_grad.7 = bf16[4,3,80,1120]{3,2,1,0:T(8,128)(2,1)} custom-call(s32[1]{0:T(128)} %bitcast.20.info, bf16[2,4,160,512]{3,2,1,0:T(8,128)(2,1)} %bitcast.91, bf16[4,320,512]{2,1,0:T(8,128)(2,1)} %all-to-all-done.16.refs_0_, bf16[4,320,512]{2,1,0:T(8,128)(2,1)} %collective-permute-done.24.refs_1_), custom_call_target="tpu_custom_call" | custom-call | flops 8808038400 | bytes 3932160 | tf_op jit(solution)/shard_map/weight_grad/pallas_call | solution.py:504
  455.7 13.4 %backward_conv.9 = (bf16[2,2,4,80,512]{4,3,2,1,0:T(8,128)(2,1)}, f32[512,512]{1,0:T(8,128)}, f32[32,8,128]{2,1,0:T(8,128)}, f32[4,8,512]{2,1,0:T(8,128)}, f32[4,8,512]{2,1,0:T(8,128)}, /*index=5*/f32[1,1280]{1,0:T(1,128)}) custom-call(s32[12]{0:T(128)} %pad_add_fusion.1.refs_0_.info, f32[640,512]{1,0:T(8,128)} %get-tuple-element.295.up, ...), custom_call_target="tpu_custom_call" | custom-call | flops 7046430720 | bytes 13762560 | tf_op jit(solution)/shard_map/backward_conv/pallas_call | solution.py:402
  473.5 5.7 convolution_multiply_fusion
  479.2 16.3 %weight_grad.8 = bf16[4,3,80,1120]{3,2,1,0:T(8,128)(2,1)} custom-call(s32[1]{0:T(128)} %bitcast.20.info, bf16[2,4,160,512]{3,2,1,0:T(8,128)(2,1)} %bitcast.90, bf16[4,320,512]{2,1,0:T(8,128)(2,1)} %all-to-all-done.18.refs_0_, bf16[4,320,512]{2,1,0:T(8,128)(2,1)} %collective-permute-done.25.refs_1_), custom_call_target="tpu_custom_call" | custom-call | flops 8808038400 | bytes 3932160 | tf_op jit(solution)/shard_map/weight_grad/pallas_call | solution.py:504
  496.5 4.8 all-to-all-start.20
  501.4 13.0 %weight_grad.9 = bf16[4,3,80,896]{3,2,1,0:T(8,128)(2,1)} custom-call(s32[1]{0:T(128)} %bitcast.20.info, bf16[2,4,128,512]{3,2,1,0:T(8,128)(2,1)} %bitcast.94, bf16[4,320,512]{2,1,0:T(8,128)(2,1)} %all-to-all-done.19.refs_0_, bf16[4,320,512]{2,1,0:T(8,128)(2,1)} %collective-permute-done.26.refs_1_), custom_call_target="tpu_custom_call" | custom-call | flops 7046430720 | bytes 3670016 | tf_op jit(solution)/shard_map/weight_grad/pallas_call | solution.py:504
  518.9 30.3 %collective-permute-done.28 = bf16[3,80,896]{2,1,0:T(8,128)(2,1)S(1)} collective-permute-done((bf16[3,80,896]{2,1,0:T(8,128)(2,1)S(1)}, bf16[3,80,896]{2,1,0:T(8,128)(2,1)S(1)}, u32[]{:S(2)}, u32[]{:S(2)}) %collective-permute-start.28) | collective-permute-done | bytes 430112 | tf_op jit(solution)/shard_map/ppermute | solution.py:787
  559.7 18.8 %collective-permute-done.27.refs_1_ = bf16[3,80,896]{2,1,0:T(8,128)(2,1)} collective-permute-done((bf16[3,80,896]{2,1,0:T(8,128)(2,1)}, bf16[3,80,896]{2,1,0:T(8,128)(2,1)}, u32[]{:S(2)}, u32[]{:S(2)}) %collective-permute-start.27) | collective-permute-done | bytes 430112 | tf_op jit(solution)/shard_map/ppermute | solution.py:788
  (214 shorter events, 198.9 us)
Async XLA Ops:
  34.0 18.1 %all-to-all-start = ((f32[32,16,128]{2,1,0:T(8,128)}), f32[32,16,128]{2,1,0:T(8,128)S(1)}, u32[]{:S(2)}, u32[]{:S(2)}) async-start(f32[32,16,128]{2,1,0:T(8,128)} %get-tuple-element.166), calls=%async_computation | async-start | bytes 524288 | tf_op jit(solution)/shard_map/all_to_all | solution.py:700
  52.1 26.4 %all-to-all-start.1 = ((bf16[4,128,512]{2,1,0:T(8,128)(2,1)}), bf16[4,128,512]{2,1,0:T(8,128)(2,1)}, u32[]{:S(2)}, u32[]{:S(2)}) async-start(bf16[4,128,512]{2,1,0:T(8,128)(2,1)} %bitcast.81), calls=%async_computation.1 | async-start | bytes 1048576 | tf_op jit(solution)/shard_map/all_to_all | solution.py:750
  73.6 17.1 %collective-permute-start.4 = (f32[4,8,640]{2,1,0:T(8,128)}, f32[4,8,640]{2,1,0:T(8,128)}, u32[]{:S(2)}, u32[]{:S(2)}) collective-permute-start(f32[4,8,640]{2,1,0:T(8,128)} %get-tuple-element.177), channel_id=1, source_target_pairs={{0,1},{1,2},{2,3},{4,5},{5,6},{6,7},{8,9},{9,10},{10,11},{12,13},{... | collective-permute-start | bytes 245768 | tf_op jit(solution)/shard_map/ppermute | solution.py:694
  78.4 16.3 %all-to-all-start.2 = ((f32[32,16,128]{2,1,0:T(8,128)}), f32[32,16,128]{2,1,0:T(8,128)S(1)}, u32[]{:S(2)}, u32[]{:S(2)}) async-start(f32[32,16,128]{2,1,0:T(8,128)} %get-tuple-element.176), calls=%async_computation.2 | async-start | bytes 524288 | tf_op jit(solution)/shard_map/all_to_all | solution.py:700
  84.1 68.6 %all-gather.11.cloned.1.call-start = ((), (), s32[]{:S(2)}) async-start(), calls=%async_computation.31 | async-start | bytes 1572864 | tf_op jit(solution)/shard_map/all_gather | solution.py:753
  94.7 22.0 %all-to-all-start.3 = ((bf16[4,160,512]{2,1,0:T(8,128)(2,1)}), bf16[4,160,512]{2,1,0:T(8,128)(2,1)}, u32[]{:S(2)}, u32[]{:S(2)}) async-start(bf16[4,160,512]{2,1,0:T(8,128)(2,1)} %bitcast.76), calls=%async_computation.3 | async-start | bytes 1310720 | tf_op jit(solution)/shard_map/all_to_all | solution.py:750
  120.3 69.0 %all-gather.13.cloned.1.call-start = ((), (), s32[]{:S(2)}) async-start(), calls=%async_computation.32 | async-start | bytes 1966080 | tf_op jit(solution)/shard_map/all_gather | solution.py:753
  131.0 21.7 %all-to-all-start.5 = ((bf16[4,160,512]{2,1,0:T(8,128)(2,1)}), bf16[4,160,512]{2,1,0:T(8,128)(2,1)}, u32[]{:S(2)}, u32[]{:S(2)}) async-start(bf16[4,160,512]{2,1,0:T(8,128)(2,1)} %bitcast.75), calls=%async_computation.5 | async-start | bytes 1310720 | tf_op jit(solution)/shard_map/all_to_all | solution.py:750
  156.4 54.0 %all-gather.15.cloned.1.call-start = ((), (), s32[]{:S(2)}) async-start(), calls=%async_computation.33 | async-start | bytes 1966080 | tf_op jit(solution)/shard_map/all_gather | solution.py:753
  167.1 22.2 %all-to-all-start.7 = ((bf16[4,160,512]{2,1,0:T(8,128)(2,1)}), bf16[4,160,512]{2,1,0:T(8,128)(2,1)}, u32[]{:S(2)}, u32[]{:S(2)}) async-start(bf16[4,160,512]{2,1,0:T(8,128)(2,1)} %bitcast.74), calls=%async_computation.7 | async-start | bytes 1310720 | tf_op jit(solution)/shard_map/all_to_all | solution.py:750
  228.8 69.1 %all-gather.17.cloned.1.call-start = ((), (), s32[]{:S(2)}) async-start(), calls=%async_computation.34 | async-start | bytes 1966080 | tf_op jit(solution)/shard_map/all_gather | solution.py:753
  257.6 41.6 %all-gather.19.cloned.1.call-start = ((), (), s32[]{:S(2)}) async-start(), calls=%async_computation.35 | async-start | bytes 1966080 | tf_op jit(solution)/shard_map/all_gather | solution.py:753
  269.0 28.8 %all-to-all-start.12 = ((bf16[4,320,512]{2,1,0:T(8,128)(2,1)}), bf16[4,320,512]{2,1,0:T(8,128)(2,1)}, u32[]{:S(2)}, u32[]{:S(2)}) async-start(bf16[4,320,512]{2,1,0:T(8,128)(2,1)} %bitcast.67), calls=%async_computation.12 | async-start | bytes 2621440 | tf_op jit(solution)/shard_map/all_to_all | solution.py:766
  273.4 222.2 %reduce-scatter.6.cloned.1.call-start = ((), (), s32[]{:S(2)}) async-start(), calls=%async_computation.26 | async-start | bytes 4096000 | tf_op jit(solution)/shard_map/reduce_scatter | solution.py:900
  299.3 15.5 %collective-permute-start.18 = (bf16[4,320,512]{2,1,0:T(8,128)(2,1)}, bf16[4,320,512]{2,1,0:T(8,128)(2,1)}, u32[]{:S(2)}, u32[]{:S(2)}) collective-permute-start(bf16[4,320,512]{2,1,0:T(8,128)(2,1)} %all-to-all-done.12.refs_0_), channel_id=1, source_target_pairs={{0,1},{1,0},{2,3},{3,2},{4,5},{5,4},{6,7},{7,6},{8,9},{9,8},{10,11... | collective-permute-start | bytes 3932168 | tf_op jit(solution)/shard_map/ppermute | solution.py:769
  299.4 15.4 %all-to-all-start.13 = ((f32[32,16,128]{2,1,0:T(8,128)}), f32[32,16,128]{2,1,0:T(8,128)S(1)}, u32[]{:S(2)}, u32[]{:S(2)}) async-start(f32[32,16,128]{2,1,0:T(8,128)} %get-tuple-element.255), calls=%async_computation.13 | async-start | bytes 524288 | tf_op jit(solution)/shard_map/all_to_all | solution.py:700
  304.1 247.3 %reduce-scatter.14.cloned.1.call-start = ((), (), s32[]{:S(2)}) async-start(), calls=%async_computation.30 | async-start | bytes 2764800 | tf_op jit(solution)/shard_map/reduce_scatter | solution.py:794
  331.1 22.8 %all-to-all-start.14 = ((bf16[4,320,512]{2,1,0:T(8,128)(2,1)}), bf16[4,320,512]{2,1,0:T(8,128)(2,1)}, u32[]{:S(2)}, u32[]{:S(2)}) async-start(bf16[4,320,512]{2,1,0:T(8,128)(2,1)} %bitcast.65), calls=%async_computation.14 | async-start | bytes 2621440 | tf_op jit(solution)/shard_map/all_to_all | solution.py:766
  353.9 20.7 %collective-permute-start.21 = (bf16[4,320,512]{2,1,0:T(8,128)(2,1)}, bf16[4,320,512]{2,1,0:T(8,128)(2,1)}, u32[]{:S(2)}, u32[]{:S(2)}) collective-permute-start(bf16[4,320,512]{2,1,0:T(8,128)(2,1)} %all-to-all-done.14.refs_0_), channel_id=1, source_target_pairs={{0,1},{1,0},{2,3},{3,2},{4,5},{5,4},{6,7},{7,6},{8,9},{9,8},{10,11... | collective-permute-start | bytes 3932168 | tf_op jit(solution)/shard_map/ppermute | solution.py:769
  353.9 20.7 %all-to-all-start.15 = ((f32[32,16,128]{2,1,0:T(8,128)}), f32[32,16,128]{2,1,0:T(8,128)S(1)}, u32[]{:S(2)}, u32[]{:S(2)}) async-start(f32[32,16,128]{2,1,0:T(8,128)} %get-tuple-element.271), calls=%async_computation.15 | async-start | bytes 524288 | tf_op jit(solution)/shard_map/all_to_all | solution.py:700
  358.6 196.6 %reduce-scatter.12.cloned.1.call-start = ((), (), s32[]{:S(2)}) async-start(), calls=%async_computation.29 | async-start | bytes 2764800 | tf_op jit(solution)/shard_map/reduce_scatter | solution.py:794
  390.9 21.6 %all-to-all-start.16 = ((bf16[4,320,512]{2,1,0:T(8,128)(2,1)}), bf16[4,320,512]{2,1,0:T(8,128)(2,1)}, u32[]{:S(2)}, u32[]{:S(2)}) async-start(bf16[4,320,512]{2,1,0:T(8,128)(2,1)} %bitcast.66), calls=%async_computation.16 | async-start | bytes 2621440 | tf_op jit(solution)/shard_map/all_to_all | solution.py:766
  412.5 20.5 %collective-permute-start.24 = (bf16[4,320,512]{2,1,0:T(8,128)(2,1)}, bf16[4,320,512]{2,1,0:T(8,128)(2,1)}, u32[]{:S(2)}, u32[]{:S(2)}) collective-permute-start(bf16[4,320,512]{2,1,0:T(8,128)(2,1)} %all-to-all-done.16.refs_0_), channel_id=1, source_target_pairs={{0,1},{1,0},{2,3},{3,2},{4,5},{5,4},{6,7},{7,6},{8,9},{9,8},{10,11... | collective-permute-start | bytes 3932168 | tf_op jit(solution)/shard_map/ppermute | solution.py:769
  412.5 20.5 %all-to-all-start.17 = ((f32[32,16,128]{2,1,0:T(8,128)}), f32[32,16,128]{2,1,0:T(8,128)S(1)}, u32[]{:S(2)}, u32[]{:S(2)}) async-start(f32[32,16,128]{2,1,0:T(8,128)} %get-tuple-element.286), calls=%async_computation.17 | async-start | bytes 524288 | tf_op jit(solution)/shard_map/all_to_all | solution.py:700
  433.7 21.4 %all-to-all-start.18 = ((bf16[4,320,512]{2,1,0:T(8,128)(2,1)}), bf16[4,320,512]{2,1,0:T(8,128)(2,1)}, u32[]{:S(2)}, u32[]{:S(2)}) async-start(bf16[4,320,512]{2,1,0:T(8,128)(2,1)} %bitcast.68), calls=%async_computation.18 | async-start | bytes 2621440 | tf_op jit(solution)/shard_map/all_to_all | solution.py:766
  438.0 147.0 %reduce-scatter.10.cloned.1.call-start = ((), (), s32[]{:S(2)}) async-start(), calls=%async_computation.28 | async-start | bytes 2764800 | tf_op jit(solution)/shard_map/reduce_scatter | solution.py:794
  469.2 26.4 %all-to-all-start.19 = ((bf16[4,320,512]{2,1,0:T(8,128)(2,1)}), bf16[4,320,512]{2,1,0:T(8,128)(2,1)}, u32[]{:S(2)}, u32[]{:S(2)}) async-start(bf16[4,320,512]{2,1,0:T(8,128)(2,1)} %bitcast.69), calls=%async_computation.19 | async-start | bytes 2621440 | tf_op jit(solution)/shard_map/all_to_all | solution.py:766
  473.5 114.0 %reduce-scatter.8.cloned.1.call-start = ((), (), s32[]{:S(2)}) async-start(), calls=%async_computation.27 | async-start | bytes 2764800 | tf_op jit(solution)/shard_map/reduce_scatter | solution.py:794
  496.5 61.3 %all-to-all-start.20 = ((bf16[8,80,640]{2,1,0:T(8,128)(2,1)}), bf16[8,80,640]{2,1,0:T(8,128)(2,1)}, u32[]{:S(2)}, u32[]{:S(2)}) async-start(bf16[8,80,640]{2,1,0:T(8,128)(2,1)} %bitcast.72), calls=%async_computation.25 | async-start | bytes 1638400 | tf_op jit(solution)/shard_map/all_to_all | solution.py:920
  516.7 32.5 %collective-permute-start.28 = (bf16[3,80,896]{2,1,0:T(8,128)(2,1)S(1)}, bf16[3,80,896]{2,1,0:T(8,128)(2,1)S(1)}, u32[]{:S(2)}, u32[]{:S(2)}) collective-permute-start(bf16[3,80,896]{2,1,0:T(8,128)(2,1)S(1)} %get-tuple-element.326), channel_id=1, source_target_pairs={{0,8},{8,0},{1,9},{9,1},{2,10},{10,2},{3,11},{11,3},{4,12},{12,4},... | collective-permute-start | bytes 1290248 | tf_op jit(solution)/shard_map/ppermute | solution.py:787
  518.8 59.8 %collective-permute-start.27 = (bf16[3,80,896]{2,1,0:T(8,128)(2,1)}, bf16[3,80,896]{2,1,0:T(8,128)(2,1)}, u32[]{:S(2)}, u32[]{:S(2)}) collective-permute-start(bf16[3,80,896]{2,1,0:T(8,128)(2,1)} %get-tuple-element.327), channel_id=1, source_target_pairs={{0,8},{8,0},{1,9},{9,1},{2,10},{10,2},{3,11},{11,3},{4,12},{12,4},... | collective-permute-start | bytes 1290248 | tf_op jit(solution)/shard_map/ppermute | solution.py:788
  551.1 31.6 %collective-permute-start.29 = (bf16[3,80,896]{2,1,0:T(8,128)(2,1)}, bf16[3,80,896]{2,1,0:T(8,128)(2,1)}, u32[]{:S(2)}, u32[]{:S(2)}) collective-permute-start(bf16[3,80,896]{2,1,0:T(8,128)(2,1)} %fusion.4), channel_id=1, source_target_pairs={{0,16},{16,0},{1,17},{17,1},{2,18},{18,2},{3,19},{19,3},{4,20},{20... | collective-permute-start | bytes 1290248 | tf_op jit(solution)/shard_map/ppermute | solution.py:790
  (57 other events, 458.8 us)
Sparse Core Ops, SparseCore 0:
  90.8 22.5 all-gather.10
  125.2 26.9 all-gather.12
  160.7 26.9 all-gather.14
  230.8 23.0 all-gather.16
  259.7 39.5 all-gather.18
  302.2 39.7 reduce-scatter.5
  344.5 51.2 reduce-scatter.13
  398.2 49.5 reduce-scatter.11
  455.2 44.9 reduce-scatter.9
  502.5 78.8 reduce-scatter.7
